TPU v7x, 512 devices: a whole 4x8x8 slice. The times are simulated.
512 devices in a mesh: mu: 128 (over z, y, core), pa: 4 (over x).
Axes of the slice: x: 4, y: 8, z: 8, core: 2. Of those that a mesh axis runs over, the one named last changes fastest.
Arguments:
- three_center: bfloat16 [640, 64, 16384], P('mu', None, 'pa'), may hold values from -6 to 6
- pair_mu: int32 [128, 5], P('mu'), may hold values from 0 to 47
- pair_site: int32 [128, 5, 1], P('mu'), may hold values from 0 to 3; in each aligned block of 5 rows (0 to 4, 5 to 9, ..., all dimensions but the last counted through in order) at most 2 rows name the same one
- pair_pos: int32 [128, 5], P('mu'), may hold values from 0 to 11
- coeff: bfloat16 [3072, 32], replicated, may hold values from -0.21875 to 0.21875
- fitting: bfloat16 [48, 256, 256], P(None, 'pa'), as said below
Outputs:
- gfit: bfloat16 [128, 12, 1, 16384], P('mu', None, None, 'pa')
Inputs may be any that keep to these rules, and one draw needn't show every extreme that they name: `pair_site`: of the 5 pairs listed for one index of mu, at most 2 name the same site, and 2 is reached. Every fitting[b] is a symmetric matrix.
All inputs are finite; a program needn't handle non-finite values.
Results may differ from a plain program's by a relative error of at most 0.0058.
Values may be sent and summed in bfloat16 or wider, within the bound.
No kernel may reach another device: no remote copies, remote signals or barrier semaphores. Data moves between devices by JAX's collectives and lax.ppermute only.
A program may use at most 64 MiB of HBM per device.

v0:
```python
import jax
import jax.numpy as jnp
from jax import lax
from jax.sharding import PartitionSpec as P

SITES = 4
NU_SITE = 12
CAP = 2


def local(three_center, pair_mu, pair_site, pair_pos, coeff, fitting):
    mu_size = lax.axis_size("mu")
    block_size = three_center.shape[1]
    slice_width = fitting.shape[1]
    pair_count = three_center.shape[0]
    groups = mu_size // SITES
    orbitals = coeff.shape[1]
    per_group = orbitals // groups
    mu_blocks = coeff.shape[0] // block_size
    mu_rows = coeff.reshape(mu_blocks, block_size, orbitals)[pair_mu[0]]
    pieces = jnp.einsum(
        "tmo,tmx->tox", mu_rows, three_center, preferred_element_type=jnp.float32
    ).astype(jnp.bfloat16)
    columns = pieces.shape[2]
    site_ids = pair_site[0, :, 0]
    positions = pair_pos[0]
    indices = jnp.arange(pair_count, dtype=jnp.int32)
    earlier = (site_ids[:, None] == site_ids[None, :]) & (indices[:, None] > indices[None, :])
    slot_rank = jnp.sum(earlier.astype(jnp.int32), axis=1)
    slot_ids = site_ids * CAP + slot_rank
    selected = slot_ids[:, None] == jnp.arange(SITES * CAP, dtype=jnp.int32)[None, :]
    slot_keys = jnp.sum(jnp.where(selected, positions[:, None] + 1, 0), axis=0) - 1
    outgoing = jnp.einsum(
        "tk,tgx->gkx", selected.astype(jnp.bfloat16), pieces, preferred_element_type=jnp.float32
    ).astype(jnp.bfloat16)
    outgoing = outgoing.reshape(mu_size, CAP, per_group, columns)
    key_rows = jnp.tile(slot_keys.reshape(SITES, CAP), (groups, 1))
    key_grid = key_rows[:, :, None]
    arrived = lax.all_to_all(outgoing, "mu", split_axis=0, concat_axis=0, tiled=True)
    arrived_keys = lax.all_to_all(key_grid, "mu", split_axis=0, concat_axis=0, tiled=True)
    item_count = arrived.shape[2]
    flat_keys = arrived_keys[:, :, 0].reshape(-1)
    onehot = (flat_keys[None, :] == jnp.arange(NU_SITE, dtype=jnp.int32)[:, None]).astype(
        jnp.bfloat16
    )
    summed = jnp.dot(
        onehot, arrived.reshape(-1, item_count * columns), preferred_element_type=jnp.float32
    )
    fitted = summed.reshape(NU_SITE, item_count, columns).astype(jnp.bfloat16)
    my_site = lax.axis_index("mu") % SITES
    weights = lax.dynamic_index_in_dim(
        fitting.reshape(SITES, NU_SITE, slice_width, fitting.shape[2]), my_site, 0, keepdims=False
    )
    local_rows = fitted.reshape(NU_SITE, per_group, block_size, slice_width)
    partial_sum = jnp.einsum(
        "kina,kaq->kinq", local_rows, weights, preferred_element_type=jnp.float32
    )
    summed_all = lax.psum(partial_sum, "pa")
    owned_cols = lax.dynamic_slice_in_dim(
        summed_all, lax.axis_index("pa") * slice_width, slice_width, 3
    )
    result = owned_cols.reshape(NU_SITE, per_group, block_size * slice_width)
    return result.astype(jnp.bfloat16)[None]


def solution(mesh):
    in_specs = (
        P("mu", None, "pa"),
        P("mu", None),
        P("mu", None, None),
        P("mu", None),
        P(),
        P(None, "pa", None),
    )
    out_specs = P("mu", None, None, "pa")
    return jax.shard_map(local, mesh=mesh, in_specs=in_specs, out_specs=out_specs, check_vma=False)
```

profile of v0, /device:TPU:8, one launch (start us, length us, event | category | flops | bytes accessed | tf_op | source)
XLA Modules:
  0.0 134.0 jit_solution(4159100911848651290)
XLA Ops:
  0.0 0.0 copy-start
  0.0 1.0 convert_reduce_fusion
  1.0 0.7 multiply_add_fusion
  1.7 0.7 add_bitcast_fusion
  2.3 0.1 select_reduce_fusion
  2.4 0.1 sub.6
  2.5 0.6 tile.7
  3.2 17.4 %all-to-all-start = ((s32[128,2,1]{1,2,0:T(1,128)}), s32[128,2,1]{1,2,0:T(1,128)S(1)}, u32[]{:S(2)}, u32[]{:S(2)}) async-start(s32[128,2,1]{1,2,0:T(1,128)} %bitcast.2), calls=%async_computation | async-start | bytes 131072 | tf_op jit(solution)/shard_map/all_to_all | solution.py:40
  20.6 1.2 reshape.96
  21.8 0.1 copy.12
  21.9 0.7 fusion.9
  22.6 0.6 gather_fusion
  23.1 0.0 copy-done
  23.1 0.5 convolution_convert_fusion.1
  23.6 2.3 %fusion = bf16[32,8,4096]{2,1,0:T(8,128)(2,1)} fusion(bf16[5,32,4096]{2,1,0:T(8,128)(2,1)S(1)} %convolution_convert_fusion.1, s32[5]{0:T(128)S(1)} %multiply_add_fusion), kind=kOutput, calls=%fused_computation.2 | convolution fusion | flops 11534376 | bytes 3407892 | tf_op jit(solution)/shard_map/tk,tgx->gkx/dot_general | solution.py:33
  25.9 4.4 %reshape.97 = bf16[128,2,1,4096]{3,1,0,2:T(2,128)(2,1)} reshape(bf16[32,8,4096]{2,1,0:T(8,128)(2,1)} %fusion) | data formatting | bytes 4194304 | tf_op jit(solution)/shard_map/reshape | solution.py:36
  30.3 1.0 all-to-all-done
  31.3 13.2 %all-to-all-start.1 = ((bf16[128,2,1,4096]{3,1,2,0:T(2,128)(2,1)}), bf16[128,2,1,4096]{3,1,2,0:T(2,128)(2,1)}, u32[]{:S(2)}, u32[]{:S(2)}) async-start(bf16[128,2,1,4096]{3,1,2,0:T(2,128)(2,1)} %bitcast.34), calls=%async_computation.1 | async-start | bytes 4194304 | tf_op jit(solution)/shard_map/all_to_all | solution.py:39
  44.5 0.5 broadcast.68
  45.0 0.8 reduce.3
  45.9 0.1 eq.49
  46.0 52.2 %all-to-all-done.1 = bf16[128,2,1,4096]{3,1,2,0:T(2,128)(2,1)} async-done(((bf16[128,2,1,4096]{3,1,2,0:T(2,128)(2,1)}), bf16[128,2,1,4096]{3,1,2,0:T(2,128)(2,1)}, u32[]{:S(2)}, u32[]{:S(2)}) %all-to-all-start.1) | async-done | bytes 2097184 | tf_op jit(solution)/shard_map/all_to_all | solution.py:39
  98.2 4.1 %reshape.98 = bf16[256,4096]{1,0:T(8,128)(2,1)} reshape(bf16[128,2,1,4096]{3,1,2,0:T(2,128)(2,1)} %all-to-all-done.1) | data formatting | bytes 4194304 | tf_op jit(solution)/shard_map/reshape | solution.py:47
  102.3 2.0 %convolution_convert_fusion.2 = bf16[12,4096]{1,0:T(8,128)(2,1)S(1)} fusion(bf16[256,4096]{1,0:T(8,128)(2,1)} %reshape.98, s32[256]{0:T(256)S(1)} %eq.49), kind=kOutput, calls=%fused_computation.4 | convolution fusion | flops 25218048 | bytes 2196480 | tf_op jit(solution)/shard_map/dot_general | solution.py:46
  104.3 0.9 reshape.99
  105.2 1.3 %convolution_bitcast_fusion = f32[12,1,64,256]{3,2,0,1:T(8,128)S(1)} fusion(bf16[12,64,64]{2,1,0:T(8,128)(2,1)} %reshape.99, bf16[4,12,64,256]{3,2,1,0:T(8,128)(2,1)} %bitcast.35, s32[]{:T(128)S(6)} %select_n.31), kind=kOutput, calls=%fused_computation.6 | convolution fusion | flops 25165824 | bytes 1376260 | tf_op jit(solution)/shard_map/kina,kaq->kinq/dot_general | solution.py:55
  106.5 25.6 %all-reduce.1 = bf16[12,1,64,256]{3,2,0,1:T(8,128)(2,1)} all-reduce(f32[12,1,64,256]{3,2,0,1:T(8,128)S(1)} %convolution_bitcast_fusion), channel_id=1, replica_groups=mesh['mu'=128,'pa'=4] {'pa'}, use_global_device_ids=true, to_apply=%region_2.3 | all-reduce | flops 196608 | bytes 1179648 | tf_op jit(solution)/shard_map/psum | solution.py:58
  132.1 1.0 dynamic-slice_convert_fusion
  133.2 0.8 convert_element_type.39
  (2 shorter events, 0.0 us)
Async XLA Ops:
  0.0 23.1 %copy-start = (bf16[5,64,4096]{2,1,0:T(8,128)(2,1)S(1)}, bf16[5,64,4096]{2,1,0:T(8,128)(2,1)}, u32[]{:S(2)}) copy-start(bf16[5,64,4096]{2,1,0:T(8,128)(2,1)} %param.6) | copy-start | bytes 7864324
  3.2 28.1 %all-to-all-start = ((s32[128,2,1]{1,2,0:T(1,128)}), s32[128,2,1]{1,2,0:T(1,128)S(1)}, u32[]{:S(2)}, u32[]{:S(2)}) async-start(s32[128,2,1]{1,2,0:T(1,128)} %bitcast.2), calls=%async_computation | async-start | bytes 131072 | tf_op jit(solution)/shard_map/all_to_all | solution.py:40
  31.3 66.9 %all-to-all-start.1 = ((bf16[128,2,1,4096]{3,1,2,0:T(2,128)(2,1)}), bf16[128,2,1,4096]{3,1,2,0:T(2,128)(2,1)}, u32[]{:S(2)}, u32[]{:S(2)}) async-start(bf16[128,2,1,4096]{3,1,2,0:T(2,128)(2,1)} %bitcast.34), calls=%async_computation.1 | async-start | bytes 4194304 | tf_op jit(solution)/shard_map/all_to_all | solution.py:39
where the time goes:
time: 135 us; the launch traced here: 134 us
  waiting for transfers between devices  53.2 us (39%)
  starting transfers between devices  30.6 us (23%)
  blocking collectives  25.6 us (19%)
  local copies, waits for them, and re-layouts  14.6 us (11%)
  matrix products  6.07 us (4%)
  other arithmetic  3.92 us (3%)
    all_to_all x1, waiting for transfers between devices, local(): lax.all_to_all(outgoing, 'mu', split_axis=0, concat_axis=0, tiled=True)  52.2 us
    psum x1, blocking collectives, local(): summed_all = lax.psum(partial_sum, 'pa')  25.6 us
    all_to_all x1, starting transfers between devices, local(): lax.all_to_all(key_grid, 'mu', split_axis=0, concat_axis=0, tiled=True)  17.4 us
    all_to_all x1, starting transfers between devices, local(): lax.all_to_all(outgoing, 'mu', split_axis=0, concat_axis=0, tiled=True)  13.2 us
    reshape x1, local copies, waits for them, and re-layouts, local(): outgoing = outgoing.reshape(mu_size, CAP, per_group, columns)  4.4 us
    reshape x1, local copies, waits for them, and re-layouts, local(): arrived.reshape(-1, item_count * columns)  4.12 us
  transfers between devices with their start and end apart: 2, of which 2 were waited for; matrix products, arithmetic and copies ran while one was open for 8% of the time, Pallas kernels for 0%

commit v1 on v0

v1 whole, which is shorter than its diff:
```python
import jax
import jax.numpy as jnp
from jax import lax
from jax.experimental import pallas as pl
from jax.experimental.pallas import tpu as pltpu
from jax.sharding import Mesh, PartitionSpec as P

SITES = 4
NU_SITE = 12
NT = 5
BS = 64
NOB = 32
LANES = 128
NSRC = 128
BUCKETS = SITES * NU_SITE
BLK = 1024
SUB = BLK // LANES
UNIT = NT * SUB
ALL_MU = ("yl", "c", "z", "yh")
FIT = ("x", "yl", "c")


def piece_kernel(mu_ref, slab_ref, *refs):
    coeff_refs, out_ref, scr = refs[:NT], refs[NT], refs[NT + 1]
    for t in range(NT):
        res = lax.dot_general(
            coeff_refs[t][...],
            slab_ref[t],
            (((0,), (0,)), ((), ())),
            preferred_element_type=jnp.float32,
        )
        for j in range(SUB):
            scr[pl.ds(t * SUB + j, NOB, stride=UNIT), :] = res[:, j * LANES : (j + 1) * LANES]
    out_ref[...] = scr[...].astype(jnp.bfloat16)


def make_pieces(three_center, mu_list, coeff):
    def coeff_map(t):
        return lambda q, mu: (mu[t], 0)

    return pl.pallas_call(
        piece_kernel,
        grid_spec=pltpu.PrefetchScalarGridSpec(
            num_scalar_prefetch=1,
            grid=(SITES,),
            in_specs=[pl.BlockSpec((NT, BS, BLK), lambda q, mu: (0, 0, q))]
            + [pl.BlockSpec((BS, NOB), coeff_map(t)) for t in range(NT)],
            out_specs=pl.BlockSpec((NOB * UNIT, LANES), lambda q, mu: (q, 0)),
            scratch_shapes=[pltpu.VMEM((NOB * UNIT, LANES), jnp.float32)],
        ),
        out_shape=jax.ShapeDtypeStruct((SITES * NOB * UNIT, LANES), jnp.bfloat16),
        compiler_params=pltpu.CompilerParams(vmem_limit_bytes=32 * 2**20),
        cost_estimate=pl.CostEstimate(
            flops=2 * NT * BS * NOB * 4096, bytes_accessed=4 * 2**20, transcendentals=0
        ),
        name="pieces",
    )(mu_list, three_center, *([coeff] * NT))


NACC = 4


def sum_kernel(key_ref, in_ref, out_ref, *accs):
    for acc in accs:
        acc[...] = jnp.zeros_like(acc)

    @pl.loop(0, NSRC * NT // 16)
    def _(i):
        for pair in range(8):
            two = in_ref[pl.ds(pl.multiple_of(i * (16 * SUB) + pair * 16, 16), 16), :].astype(jnp.float32)
            for half in range(2):
                acc = accs[(pair * 2 + half) % NACC]
                row = key_ref[i * 16 + pair * 2 + half] * SUB
                where = pl.ds(pl.multiple_of(row, SUB), SUB)
                acc[where, :] = acc[where, :] + two[half * SUB : (half + 1) * SUB]

    total = accs[0][...]
    for acc in accs[1:]:
        total = total + acc[...]
    total = total.astype(jnp.bfloat16)
    for x in range(4):
        out_ref[x] = total


def make_sums(keys, arrived):
    return pl.pallas_call(
        sum_kernel,
        in_specs=[
            pl.BlockSpec(memory_space=pltpu.SMEM),
            pl.BlockSpec(memory_space=pltpu.VMEM),
        ],
        out_specs=pl.BlockSpec(memory_space=pltpu.VMEM),
        out_shape=jax.ShapeDtypeStruct((4, BUCKETS * SUB, LANES), jnp.bfloat16),
        scratch_shapes=[pltpu.VMEM((BUCKETS * SUB, LANES), jnp.float32)] * NACC,
        compiler_params=pltpu.CompilerParams(vmem_limit_bytes=32 * 2**20),
        cost_estimate=pl.CostEstimate(
            flops=NSRC * NT * BLK, bytes_accessed=2 * 2**20, transcendentals=0
        ),
        name="sums",
    )(keys, arrived)


def fit_kernel(in_ref, weight_ref, out_ref):
    for k in range(NU_SITE):
        rows = [
            jnp.concatenate([in_ref[x, q, pl.ds(k * SUB, SUB), :] for q in range(4)], axis=0)
            for x in range(4)
        ]
        left = jnp.concatenate(rows, axis=1)
        res = lax.dot_general(
            left, weight_ref[k], (((1,), (1,)), ((), ())), preferred_element_type=jnp.float32
        )
        out_ref[k] = res.astype(jnp.bfloat16)


def make_fit(gathered, weights):
    return pl.pallas_call(
        fit_kernel,
        in_specs=[pl.BlockSpec(memory_space=pltpu.VMEM)] * 2,
        out_specs=pl.BlockSpec(memory_space=pltpu.VMEM),
        out_shape=jax.ShapeDtypeStruct((NU_SITE, 32, LANES), jnp.bfloat16),
        compiler_params=pltpu.CompilerParams(vmem_limit_bytes=32 * 2**20),
        name="fit",
    )(gathered, weights)


def local(three_center, pair_mu, pair_site, pair_pos, coeff, fitting):
    keys = pair_site[:, :, 0] * NU_SITE + pair_pos
    keys = jnp.pad(keys, ((0, 0), (0, LANES - NT)))
    all_keys = lax.all_gather(keys, ALL_MU, axis=0, tiled=True)
    all_keys = all_keys[:, :NT].reshape(-1)
    pieces = make_pieces(three_center, pair_mu[0], coeff)
    arrived = lax.all_to_all(pieces, ALL_MU, split_axis=0, concat_axis=0, tiled=True)
    site = lax.axis_index("yl") * 2 + lax.axis_index("c")
    weights = lax.dynamic_slice_in_dim(fitting, site * NU_SITE, NU_SITE, 0)
    same = jnp.eye(2, dtype=jnp.bfloat16)
    weights = weights.reshape(NU_SITE, 1, 64, 4, 1, 64) * same.reshape(1, 2, 1, 1, 2, 1)
    weights = weights.reshape(NU_SITE, LANES, 4 * LANES)
    sums = make_sums(all_keys, arrived)
    gathered = lax.all_to_all(
        sums.reshape(16, NU_SITE * SUB, LANES), FIT, split_axis=0, concat_axis=0, tiled=True
    )
    result = make_fit(gathered.reshape(4, 4, NU_SITE * SUB, LANES), weights)
    return result.reshape(1, NU_SITE, 1, 4096)


def solution(mesh):
    fine = Mesh(mesh.devices.reshape(8, 4, 2, 2, 4), ("z", "yh", "yl", "c", "x"))
    mu = ("z", "yh", "yl", "c")
    in_specs = (
        P(mu, None, "x"),
        P(mu, None),
        P(mu, None, None),
        P(mu, None),
        P(),
        P(None, "x", None),
    )
    out_specs = P(mu, None, None, "x")
    return jax.shard_map(local, mesh=fine, in_specs=in_specs, out_specs=out_specs, check_vma=False)
```

time: 135 us -> 378 us (2.80)
  the two profiles are of different devices: /device:TPU:8 before, /device:TPU:1 now
where the time goes in v1:
time: 378 us
  blocking collectives  306 us (81%)
  starting transfers between devices  43.5 us (12%)
  local copies, waits for them, and re-layouts  22 us (6%)
  Pallas kernels  4.54 us (1%)
    all_gather x1, blocking collectives, local(): all_keys = lax.all_gather(keys, ALL_MU, axis=0, tiled=True)  306 us
    all_to_all x1, starting transfers between devices, local(): lax.all_to_all(sums.reshape(16, NU_SITE * SUB, LANES), FIT, split_axis=0,...  24.9 us
    all_to_all x1, starting transfers between devices, local(): lax.all_to_all(pieces, ALL_MU, split_axis=0, concat_axis=0, tiled=True)  18.7 us
    mul x5, local copies, waits for them, and re-layouts, local(): weights.reshape(NU_SITE, 1, 64, 4, 1, 64) * same.reshape(1, 2, 1, 1, 2, 1)  13.8 us
  transfers between devices with their start and end apart: 2, of which 0 were waited for; matrix products, arithmetic and copies ran while one was open for 4% of the time, Pallas kernels for 0%

profile of v1, /device:TPU:1, one launch (start us, length us, event | category | flops | bytes accessed | tf_op | source)
XLA Modules:
  0.0 377.8 jit_solution(5831387367489497683)
XLA Ops:
  0.0 0.0 copy-start
  0.0 1.4 copy.17.refs_0_.refs_1_.refs_2_.refs_3_.refs_4_
  1.4 0.0 copy-start.2
  1.4 1.7 copy-done.2
  3.2 0.0 copy-start.5
  3.2 0.7 copy-done.5
  3.8 2.1 pieces.1
  5.9 0.0 copy-start.1
  5.9 1.1 copy-done.1
  7.0 0.0 copy-start.6
  7.0 0.0 copy-start.7
  7.0 18.7 %all-to-all-start = ((bf16[128,40,128]{2,1,0:T(8,128)(2,1)}), bf16[128,40,128]{2,1,0:T(8,128)(2,1)S(1)}, u32[]{:S(2)}, u32[]{:S(2)}) async-start(bf16[128,40,128]{2,1,0:T(8,128)(2,1)} %bitcast.12), calls=%async_computation | async-start | bytes 2621440 | tf_op jit(solution)/shard_map/all_to_all | solution.py:133
  25.7 0.0 copy-done.6
  25.7 0.0 copy-done.7
  25.7 306.0 %all-gather = s32[128,1,128]{2,1,0:T(1,128)S(1)} all-gather(s32[1,1,128]{2,1,0:T(1,128)S(1)} %pad_bitcast_fusion), channel_id=1, replica_groups=mesh['z'=8,'yh'=4,'yl'=2,'c'=2,'x'=4] {'yl','c','z','yh'}, dimensions={0}, use_global_device_ids=true | all-gather | bytes 66048 | tf_op jit(solution)/shard_map/all_gather | solution.py:130
  331.8 0.2 reshape.42.key_ref
  332.0 0.0 all-to-all-done
  332.0 1.9 sums.1
  333.8 0.0 copy-start.3
  333.8 0.7 copy-done.3
  334.6 24.9 %all-to-all-start.1 = ((bf16[16,96,128]{2,1,0:T(8,128)(2,1)}), bf16[16,96,128]{2,1,0:T(8,128)(2,1)S(1)}, u32[]{:S(2)}, u32[]{:S(2)}) async-start(bf16[16,96,128]{2,1,0:T(8,128)(2,1)} %bitcast.14), calls=%async_computation.1 | async-start | bytes 786432 | tf_op jit(solution)/shard_map/all_to_all | solution.py:140
  359.5 0.0 copy-done
  359.5 0.3 mul.46
  359.8 4.4 %mul.47 = bf16[12,2,64,4,2,64]{5,4,3,2,1,0:T(2,128)(2,1)} broadcast(bf16[12,64,4,64]{3,2,1,0:T(4,128)(2,1)S(1)} %mul.46), dimensions={0,2,3,5} | broadcast | bytes 1966080 | tf_op jit(solution)/shard_map/mul | solution.py:137
  364.3 8.0 %mul.48 = bf16[12,128,512]{2,1,0:T(8,128)(2,1)} reshape(bf16[12,2,64,4,2,64]{5,4,3,2,1,0:T(2,128)(2,1)} %mul.47) | data formatting | bytes 3145728 | tf_op jit(solution)/shard_map/mul | solution.py:137
  372.3 0.2 mul.49
  372.5 0.9 mul.50
  373.3 1.5 broadcast_multiply_fusion.weight_ref
  374.9 0.0 all-to-all-done.1
  374.9 0.6 fit.1
  375.5 0.0 copy-start.4
  375.5 0.6 copy-done.4
  376.1 1.6 reshape.45
  (4 shorter events, 0.0 us)
Async XLA Ops:
  0.0 359.5 %copy-start = (bf16[48,64,256]{2,1,0:T(8,128)(2,1)S(1)}, bf16[48,64,256]{2,1,0:T(8,128)(2,1)}, u32[]{:S(2)}) copy-start(bf16[48,64,256]{2,1,0:T(8,128)(2,1)} %param.11) | copy-start | bytes 4718596
  1.4 1.7 copy-start.2
  3.2 0.7 copy-start.5
  5.9 1.1 copy-start.1
  7.0 18.7 %copy-start.6 = (s32[1,5]{1,0:T(1,128)S(1)}, s32[1,5]{1,0:T(1,128)}, u32[]{:S(2)}) copy-start(s32[1,5]{1,0:T(1,128)} %param.9) | copy-start | bytes 64
  7.0 18.7 %copy-start.7 = (s32[1,5,1]{1,2,0:T(1,128)S(1)}, s32[1,5,1]{1,2,0:T(1,128)}, u32[]{:S(2)}) copy-start(s32[1,5,1]{1,2,0:T(1,128)} %param.8) | copy-start | bytes 64
  7.0 325.0 %all-to-all-start = ((bf16[128,40,128]{2,1,0:T(8,128)(2,1)}), bf16[128,40,128]{2,1,0:T(8,128)(2,1)S(1)}, u32[]{:S(2)}, u32[]{:S(2)}) async-start(bf16[128,40,128]{2,1,0:T(8,128)(2,1)} %bitcast.12), calls=%async_computation | async-start | bytes 2621440 | tf_op jit(solution)/shard_map/all_to_all | solution.py:133
  333.8 0.8 copy-start.3
  334.6 40.3 %all-to-all-start.1 = ((bf16[16,96,128]{2,1,0:T(8,128)(2,1)}), bf16[16,96,128]{2,1,0:T(8,128)(2,1)S(1)}, u32[]{:S(2)}, u32[]{:S(2)}) async-start(bf16[16,96,128]{2,1,0:T(8,128)(2,1)} %bitcast.14), calls=%async_computation.1 | async-start | bytes 786432 | tf_op jit(solution)/shard_map/all_to_all | solution.py:140
  375.5 0.7 copy-start.4

commit v2 on v1

v2 whole, which is shorter than its diff:
```python
import jax
import jax.numpy as jnp
from jax import lax
from jax.experimental import pallas as pl
from jax.experimental.pallas import tpu as pltpu
from jax.sharding import Mesh, PartitionSpec as P

SITES = 4
NU_SITE = 12
NT = 5
BS = 64
NOB = 32
LANES = 128
NSRC = 128
BUCKETS = SITES * NU_SITE
BLK = 1024
SUB = BLK // LANES
UNIT = (NT + 1) * SUB
ALL_MU = ("yl", "c", "z", "yh")
FIT = ("x", "yl", "c")
MIB = 2**20


def piece_kernel(mu_ref, site_ref, pos_ref, row_ref, slab_ref, *refs):
    coeff_refs, out_ref, scr = refs[:NT], refs[NT], refs[NT + 1]

    @pl.when(pl.program_id(0) == 0)
    def _():
        lane = lax.broadcasted_iota(jnp.int32, (SUB, LANES), 1)
        row = lax.broadcasted_iota(jnp.int32, (SUB, LANES), 0)
        tile = jnp.zeros((SUB, LANES), jnp.int32)
        for t in range(NT):
            tile = jnp.where(lane == t, site_ref[t] * NU_SITE + pos_ref[t], tile)
        tile = jnp.where(row == row_ref[0], tile, 0).astype(jnp.float32)
        for o in range(NOB):
            scr[o * UNIT + NT * SUB : (o + 1) * UNIT, :] = tile

    for t in range(NT):
        both = coeff_refs[t][...].astype(jnp.float32)
        mine = jnp.where(mu_ref[t] % 2 == 1, both[:, BS:], both[:, :BS]).astype(jnp.bfloat16)
        res = jnp.dot(mine, slab_ref[t], preferred_element_type=jnp.float32)
        for j in range(SUB):
            scr[pl.ds(t * SUB + j, NOB, stride=UNIT), :] = res[:, j * LANES : (j + 1) * LANES]
    out_ref[...] = scr[...].astype(jnp.bfloat16)


def make_pieces(three_center, pair_mu, pair_site, pair_pos, row, coeff):
    def coeff_map(t):
        return lambda q, mu, site, pos, row: (0, mu[t] // 2)

    return pl.pallas_call(
        piece_kernel,
        grid_spec=pltpu.PrefetchScalarGridSpec(
            num_scalar_prefetch=4,
            grid=(SITES,),
            in_specs=[pl.BlockSpec((NT, BS, BLK), lambda q, *_: (0, 0, q))]
            + [pl.BlockSpec((NOB, 2 * BS), coeff_map(t)) for t in range(NT)],
            out_specs=pl.BlockSpec((NOB * UNIT, LANES), lambda q, *_: (q, 0)),
            scratch_shapes=[pltpu.VMEM((NOB * UNIT, LANES), jnp.float32)],
        ),
        out_shape=jax.ShapeDtypeStruct((SITES * NOB * UNIT, LANES), jnp.bfloat16),
        compiler_params=pltpu.CompilerParams(vmem_limit_bytes=32 * MIB),
        cost_estimate=pl.CostEstimate(
            flops=2 * NT * BS * NOB * 4096, bytes_accessed=4 * MIB, transcendentals=0
        ),
        name="pieces",
    )(pair_mu, pair_site, pair_pos, row, three_center, *([coeff.T] * NT))


NACC = 4


def sum_kernel(in_ref, out_ref, keys_vmem, keys_smem, sem, *accs):
    for g in range(NSRC // SUB):
        tile = jnp.zeros((SUB, LANES), jnp.float32)
        for r in range(SUB):
            start = (g * SUB + r) * UNIT + NT * SUB
            tile = tile + in_ref[start - SUB : start + SUB, :].astype(jnp.float32)[SUB:]
        keys_vmem[g * SUB : (g + 1) * SUB, :] = tile.astype(jnp.int32)
    copy = pltpu.make_async_copy(keys_vmem, keys_smem, sem)
    copy.start()
    for acc in accs:
        acc[...] = jnp.zeros_like(acc)
    copy.wait()

    @pl.loop(0, NSRC // 4)
    def _(i):
        for s in range(4):
            source = i * 4 + s
            for pair in range((NT + 1) // 2):
                start = pl.multiple_of(source * UNIT + pair * 2 * SUB, 2 * SUB)
                two = in_ref[pl.ds(start, 2 * SUB), :].astype(jnp.float32)
                for half in range(2):
                    t = pair * 2 + half
                    if t < NT:
                        acc = accs[(s * NT + t) % NACC]
                        where = pl.ds(pl.multiple_of(keys_smem[source, t] * SUB, SUB), SUB)
                        acc[where, :] = acc[where, :] + two[half * SUB : (half + 1) * SUB]

    total = accs[0][...]
    for acc in accs[1:]:
        total = total + acc[...]
    total = total.astype(jnp.bfloat16)
    for x in range(4):
        out_ref[x] = total


def make_sums(arrived):
    return pl.pallas_call(
        sum_kernel,
        in_specs=[pl.BlockSpec(memory_space=pltpu.VMEM)],
        out_specs=pl.BlockSpec(memory_space=pltpu.VMEM),
        out_shape=jax.ShapeDtypeStruct((4, BUCKETS * SUB, LANES), jnp.bfloat16),
        scratch_shapes=[
            pltpu.VMEM((NSRC, LANES), jnp.int32),
            pltpu.SMEM((NSRC, LANES), jnp.int32),
            pltpu.SemaphoreType.DMA,
        ]
        + [pltpu.VMEM((BUCKETS * SUB, LANES), jnp.float32)] * NACC,
        compiler_params=pltpu.CompilerParams(vmem_limit_bytes=32 * MIB),
        cost_estimate=pl.CostEstimate(
            flops=NSRC * NT * BLK, bytes_accessed=2 * MIB, transcendentals=0
        ),
        name="sums",
    )(arrived)


HALF = LANES // 2
NHI = 32
KPAD = 16


def fit_kernel(site_ref, in_ref, weight_ref, out_ref, scr):
    for k in range(NU_SITE):
        rows = [
            jnp.concatenate([in_ref[x, q, pl.ds(k * SUB, SUB), :] for q in range(4)], axis=0)
            for x in range(4)
        ]
        low = jnp.concatenate([r[:, :HALF] for r in rows], axis=1)
        high = jnp.concatenate([r[:, HALF:] for r in rows], axis=1)
        res = lax.dot_general(
            jnp.concatenate([low, high], axis=0),
            weight_ref[k],
            (((1,), (1,)), ((), ())),
            preferred_element_type=jnp.float32,
        )
        scr[pl.ds(k, NHI, stride=KPAD), :] = jnp.concatenate([res[:NHI], res[NHI:]], axis=1)
    for n in range(NHI):
        out_ref[:, n * LANES : (n + 1) * LANES] = scr[n * KPAD : n * KPAD + NU_SITE, :].astype(
            jnp.bfloat16
        )


def make_fit(site, gathered, fitting):
    return pl.pallas_call(
        fit_kernel,
        grid_spec=pltpu.PrefetchScalarGridSpec(
            num_scalar_prefetch=1,
            grid=(1,),
            in_specs=[
                pl.BlockSpec((4, 4, NU_SITE * SUB, LANES), lambda i, site: (0, 0, 0, 0)),
                pl.BlockSpec((NU_SITE, 64, 256), lambda i, site: (site[0], 0, 0)),
            ],
            out_specs=pl.BlockSpec((NU_SITE, NHI * LANES), lambda i, site: (0, 0)),
            scratch_shapes=[pltpu.VMEM((NHI * KPAD, LANES), jnp.float32)],
        ),
        out_shape=jax.ShapeDtypeStruct((NU_SITE, NHI * LANES), jnp.bfloat16),
        compiler_params=pltpu.CompilerParams(vmem_limit_bytes=32 * MIB),
        name="fit",
    )(site, gathered, fitting)


def local(three_center, pair_mu, pair_site, pair_pos, coeff, fitting):
    row = (lax.axis_index("z") * 4 + lax.axis_index("yh")) % SUB
    pieces = make_pieces(
        three_center, pair_mu[0], pair_site[0, :, 0], pair_pos[0], row.reshape(1), coeff
    )
    arrived = lax.all_to_all(pieces, ALL_MU, split_axis=0, concat_axis=0, tiled=True)
    sums = make_sums(arrived)
    gathered = lax.all_to_all(
        sums.reshape(16, NU_SITE * SUB, LANES), FIT, split_axis=0, concat_axis=0, tiled=True
    )
    site = lax.axis_index("yl") * 2 + lax.axis_index("c")
    result = make_fit(site.reshape(1), gathered.reshape(4, 4, NU_SITE * SUB, LANES), fitting)
    return result.reshape(1, NU_SITE, 1, 4096)


def solution(mesh):
    fine = Mesh(mesh.devices.reshape(8, 4, 2, 2, 4), ("z", "yh", "yl", "c", "x"))
    mu = ("z", "yh", "yl", "c")
    in_specs = (
        P(mu, None, "x"),
        P(mu, None),
        P(mu, None, None),
        P(mu, None),
        P(),
        P(None, "x", None),
    )
    out_specs = P(mu, None, None, "x")
    return jax.shard_map(local, mesh=fine, in_specs=in_specs, out_specs=out_specs, check_vma=False)
```

time: 378 us -> 86.9 us (0.23)
  blocking collectives: 306 us -> 59.7 us
  starting transfers between devices: 43.5 us -> 6.12 us
  local copies, waits for them, and re-layouts: 22 us -> 4.63 us
  waiting for transfers between devices: 0.01 us -> 8.39 us
    all_gather x1 -> x0, blocking collectives: 306 us -> none  [local(): all_keys = lax.all_gather(keys, ALL_MU, axis=0, tiled=True)]
    all_to_all x0 -> x1, blocking collectives: none -> 59.7 us  [local(): lax.all_to_all(pieces, ALL_MU, split_axis=0, concat_axis=0, tiled=True)]
    all_to_all x1, starting transfers between devices: 24.9 us -> 6.12 us  [local(): lax.all_to_all(sums.reshape(16, NU_SITE * SUB, LANES), FIT, split_axis=0,...]
    all_to_all x1 -> x0, starting transfers between devices: 18.7 us -> none  [local(): lax.all_to_all(pieces, ALL_MU, split_axis=0, concat_axis=0, tiled=True)]
    mul x5 -> x0, local copies, waits for them, and re-layouts: 13.8 us -> none  [local(): weights.reshape(NU_SITE, 1, 64, 4, 1, 64) * same.reshape(1, 2, 1, 1, 2, 1)]
    all_to_all x1, waiting for transfers between devices: 0.01 us -> 8.39 us  [local(): lax.all_to_all(sums.reshape(16, NU_SITE * SUB, LANES), FIT, split_axis=0,...]
  transfers between devices with their start and end apart: 2 -> 1, of which waited for: 0 -> 1; matrix products, arithmetic and copies ran while one was open for 4% -> 0% of each run, Pallas kernels for 0% -> 0%
where the time goes in v2:
time: 86.9 us; the launch traced here: 86.6 us
  blocking collectives  59.7 us (69%)
  waiting for transfers between devices  8.39 us (10%)
  Pallas kernels  7.77 us (9%)
  starting transfers between devices  6.12 us (7%)
  local copies, waits for them, and re-layouts  4.63 us (5%)
    all_to_all x1, blocking collectives, local(): lax.all_to_all(pieces, ALL_MU, split_axis=0, concat_axis=0, tiled=True)  59.7 us
    all_to_all x1, waiting for transfers between devices, local(): lax.all_to_all(sums.reshape(16, NU_SITE * SUB, LANES), FIT, split_axis=0,...  8.39 us
    all_to_all x1, starting transfers between devices, local(): lax.all_to_all(sums.reshape(16, NU_SITE * SUB, LANES), FIT, split_axis=0,...  6.12 us
    unnamed x12, local copies, waits for them, and re-layouts  4.63 us
    pallas_call x1, Pallas kernels, make_sums(): pl.pallas_call(sum_kernel, in_specs=[pl.BlockSpec(memory_space=pltpu.VMEM...  3.77 us
    pallas_call x1, Pallas kernels, make_pieces(): pl.pallas_call(piece_kernel, grid_spec=pltpu.PrefetchScalarGridSpec(num_s...  2.94 us
  transfers between devices with their start and end apart: 1, of which 1 were waited for; matrix products, arithmetic and copies ran while one was open for 0% of the time, Pallas kernels for 0%

profile of v2, /device:TPU:1, one launch (start us, length us, event | category | flops | bytes accessed | tf_op | source)
XLA Modules:
  0.0 86.6 jit_solution(12488216238781321419)
XLA Ops:
  0.0 0.0 copy-start
  0.0 0.9 %copy-done = bf16[3072,32]{0,1:T(8,128)(2,1)S(1)} copy-done((bf16[3072,32]{0,1:T(8,128)(2,1)S(1)}, bf16[3072,32]{0,1:T(8,128)(2,1)}, u32[]{:S(2)}) %copy-start) | copy-done | bytes 196632
  0.9 0.0 copy-start.1
  0.9 1.7 %copy-done.1 = bf16[5,64,4096]{2,1,0:T(8,128)(2,1)S(1)} copy-done((bf16[5,64,4096]{2,1,0:T(8,128)(2,1)S(1)}, bf16[5,64,4096]{2,1,0:T(8,128)(2,1)}, u32[]{:S(2)}) %copy-start.1) | copy-done | bytes 2621464
  2.7 0.0 copy-start.3
  2.7 0.7 copy-done.3
  3.3 0.0 copy-start.4
  3.3 0.7 copy-done.4
  4.0 0.0 copy-start.5
  4.0 0.7 copy-done.5
  4.6 2.9 %pieces.1 = bf16[6144,128]{1,0:T(8,128)(2,1)S(1)} custom-call(s32[5]{0:T(128)S(1)} %bitcast.19, s32[5]{0:T(128)S(1)} %bitcast.20, s32[5]{0:T(128)S(1)} %bitcast.21, s32[1]{0:T(128)} %bitcast.4.row_ref, bf16[5,64,4096]{2,1,0:T(8,128)(2,1)S(1)} %copy-done.1, bf16[32,3072]{1,0:T(8,128)(2,1)S(1)} %bitcast.13, bf16[32,3072]{1,0:T(8,128)(2,1)S(1)} %bitcast.14, ...), custom_call_target="tpu_custom_call" | custom-call | flops 83886080 | bytes 4194304 | tf_op jit(solution)/shard_map/pieces/pallas_call | solution.py:51
  7.6 59.7 %all_to_all.16 = bf16[128,48,128]{2,1,0:T(8,128)(2,1)S(1)} all-to-all(bf16[128,48,128]{2,1,0:T(8,128)(2,1)S(1)} %bitcast.11), channel_id=1, replica_groups=mesh['z'=8,'yh'=4,'yl'=2,'c'=2,'x'=4] {'yl','c','z','yh'}, dimensions={0} | all-to-all | bytes 3145728 | tf_op jit(solution)/shard_map/all_to_all | solution.py:178
  67.3 0.0 copy-start.2
  67.3 3.8 %sums.1 = bf16[4,384,128]{2,1,0:T(8,128)(2,1)} custom-call(bf16[6144,128]{1,0:T(8,128)(2,1)S(1)} %bitcast.12), custom_call_target="tpu_custom_call" | custom-call | flops 655360 | bytes 2097152 | tf_op jit(solution)/shard_map/sums/pallas_call | solution.py:109
  71.0 6.1 %all-to-all-start.1 = ((bf16[16,96,128]{2,1,0:T(8,128)(2,1)}), bf16[16,96,128]{2,1,0:T(8,128)(2,1)S(1)}, u32[]{:S(2)}, u32[]{:S(2)}) async-start(bf16[16,96,128]{2,1,0:T(8,128)(2,1)} %bitcast.8), calls=%async_computation.1 | async-start | bytes 786432 | tf_op jit(solution)/shard_map/all_to_all | solution.py:180
  77.1 8.4 %all-to-all-done.1 = bf16[16,96,128]{2,1,0:T(8,128)(2,1)S(1)} async-done(((bf16[16,96,128]{2,1,0:T(8,128)(2,1)}), bf16[16,96,128]{2,1,0:T(8,128)(2,1)S(1)}, u32[]{:S(2)}, u32[]{:S(2)}) %all-to-all-start.1) | async-done | bytes 393248 | tf_op jit(solution)/shard_map/all_to_all | solution.py:180
  85.5 0.0 copy-done.2
  85.5 1.1 %fit.1 = bf16[12,4096]{1,0:T(8,128)(2,1)} custom-call(s32[1]{0:T(128)} %bitcast.site_ref, bf16[4,4,96,128]{3,2,1,0:T(8,128)(2,1)S(1)} %bitcast.18, bf16[48,64,256]{2,1,0:T(8,128)(2,1)S(1)} %copy-done.2), custom_call_target="tpu_custom_call" | custom-call | tf_op jit(solution)/shard_map/fit/pallas_call | solution.py:155
Async XLA Ops:
  0.0 0.9 %copy-start = (bf16[3072,32]{0,1:T(8,128)(2,1)S(1)}, bf16[3072,32]{0,1:T(8,128)(2,1)}, u32[]{:S(2)}) copy-start(bf16[3072,32]{0,1:T(8,128)(2,1)} %param.10) | copy-start | bytes 589828
  0.9 1.7 %copy-start.1 = (bf16[5,64,4096]{2,1,0:T(8,128)(2,1)S(1)}, bf16[5,64,4096]{2,1,0:T(8,128)(2,1)}, u32[]{:S(2)}) copy-start(bf16[5,64,4096]{2,1,0:T(8,128)(2,1)} %slab_ref.1) | copy-start | bytes 7864324
  2.7 0.7 copy-start.3
  3.3 0.7 copy-start.4
  4.0 0.7 copy-start.5
  67.3 18.3 %copy-start.2 = (bf16[48,64,256]{2,1,0:T(8,128)(2,1)S(1)}, bf16[48,64,256]{2,1,0:T(8,128)(2,1)}, u32[]{:S(2)}) copy-start(bf16[48,64,256]{2,1,0:T(8,128)(2,1)} %weight_ref.1) | copy-start | bytes 4718596
  71.0 14.5 %all-to-all-start.1 = ((bf16[16,96,128]{2,1,0:T(8,128)(2,1)}), bf16[16,96,128]{2,1,0:T(8,128)(2,1)S(1)}, u32[]{:S(2)}, u32[]{:S(2)}) async-start(bf16[16,96,128]{2,1,0:T(8,128)(2,1)} %bitcast.8), calls=%async_computation.1 | async-start | bytes 786432 | tf_op jit(solution)/shard_map/all_to_all | solution.py:180

commit v3 on v2

--- a/solution.py
+++ b/solution.py
@@ -11,20 +11,23 @@
 BS = 64
 NOB = 32
 LANES = 128
-NSRC = 128
+NSRC = 64
+CORES = 2
 BUCKETS = SITES * NU_SITE
 BLK = 1024
 SUB = BLK // LANES
-UNIT = (NT + 1) * SUB
-ALL_MU = ("yl", "c", "z", "yh")
+PAIR = 2 * SUB
+UNIT = NT * PAIR + SUB
+MAIN = ("yl", "z", "yh")
 FIT = ("x", "yl", "c")
 MIB = 2**20
 
 
 def piece_kernel(mu_ref, site_ref, pos_ref, row_ref, slab_ref, *refs):
     coeff_refs, out_ref, scr = refs[:NT], refs[NT], refs[NT + 1]
-
-    @pl.when(pl.program_id(0) == 0)
+    step = pl.program_id(0)
+
+    @pl.when(step == 0)
     def _():
         lane = lax.broadcasted_iota(jnp.int32, (SUB, LANES), 1)
         row = lax.broadcasted_iota(jnp.int32, (SUB, LANES), 0)
@@ -33,15 +36,26 @@
             tile = jnp.where(lane == t, site_ref[t] * NU_SITE + pos_ref[t], tile)
         tile = jnp.where(row == row_ref[0], tile, 0).astype(jnp.float32)
         for o in range(NOB):
-            scr[o * UNIT + NT * SUB : (o + 1) * UNIT, :] = tile
-
-    for t in range(NT):
-        both = coeff_refs[t][...].astype(jnp.float32)
-        mine = jnp.where(mu_ref[t] % 2 == 1, both[:, BS:], both[:, :BS]).astype(jnp.bfloat16)
-        res = jnp.dot(mine, slab_ref[t], preferred_element_type=jnp.float32)
-        for j in range(SUB):
-            scr[pl.ds(t * SUB + j, NOB, stride=UNIT), :] = res[:, j * LANES : (j + 1) * LANES]
-    out_ref[...] = scr[...].astype(jnp.bfloat16)
+            scr[o * UNIT + NT * PAIR : (o + 1) * UNIT, :] = tile
+
+    def fill(half):
+        for t in range(NT):
+            both = coeff_refs[t][...].astype(jnp.float32)
+            mine = jnp.where(mu_ref[t] % 2 == 1, both[:, BS:], both[:, :BS]).astype(jnp.bfloat16)
+            res = jnp.dot(mine, slab_ref[t], preferred_element_type=jnp.float32)
+            for j in range(SUB):
+                scr[pl.ds(t * PAIR + half * SUB + j, NOB, stride=UNIT), :] = res[
+                    :, j * LANES : (j + 1) * LANES
+                ]
+
+    @pl.when(step % 2 == 0)
+    def _():
+        fill(0)
+
+    @pl.when(step % 2 == 1)
+    def _():
+        fill(1)
+        out_ref[...] = scr[...].astype(jnp.bfloat16)
 
 
 def make_pieces(three_center, pair_mu, pair_site, pair_pos, row, coeff):
@@ -55,11 +69,11 @@
             grid=(SITES,),
             in_specs=[pl.BlockSpec((NT, BS, BLK), lambda q, *_: (0, 0, q))]
             + [pl.BlockSpec((NOB, 2 * BS), coeff_map(t)) for t in range(NT)],
-            out_specs=pl.BlockSpec((NOB * UNIT, LANES), lambda q, *_: (q, 0)),
+            out_specs=pl.BlockSpec((NOB * UNIT, LANES), lambda q, *_: (q // 2, 0)),
             scratch_shapes=[pltpu.VMEM((NOB * UNIT, LANES), jnp.float32)],
         ),
-        out_shape=jax.ShapeDtypeStruct((SITES * NOB * UNIT, LANES), jnp.bfloat16),
-        compiler_params=pltpu.CompilerParams(vmem_limit_bytes=32 * MIB),
+        out_shape=jax.ShapeDtypeStruct((2 * NOB * UNIT, LANES), jnp.bfloat16),
+        compiler_params=pltpu.CompilerParams(vmem_limit_bytes=58 * MIB),
         cost_estimate=pl.CostEstimate(
             flops=2 * NT * BS * NOB * 4096, bytes_accessed=4 * MIB, transcendentals=0
         ),
@@ -67,15 +81,19 @@
     )(pair_mu, pair_site, pair_pos, row, three_center, *([coeff.T] * NT))
 
 
-NACC = 4
-
-
-def sum_kernel(in_ref, out_ref, keys_vmem, keys_smem, sem, *accs):
+COPIES = 2
+DUO = 2 * UNIT
+
+
+def sum_kernel(core_ref, in_ref, keep_ref, send_ref, keys_vmem, keys_smem, sem, *accs):
+    tiles = UNIT // SUB
     for g in range(NSRC // SUB):
         tile = jnp.zeros((SUB, LANES), jnp.float32)
-        for r in range(SUB):
-            start = (g * SUB + r) * UNIT + NT * SUB
-            tile = tile + in_ref[start - SUB : start + SUB, :].astype(jnp.float32)[SUB:]
+        for r in range(0, SUB, 2):
+            start = (g * SUB + r) * UNIT
+            first = in_ref[start + NT * PAIR : start + NT * PAIR + PAIR, :].astype(jnp.float32)
+            second = in_ref[start + DUO - PAIR : start + DUO, :].astype(jnp.float32)
+            tile = tile + first[:SUB] + second[SUB:]
         keys_vmem[g * SUB : (g + 1) * SUB, :] = tile.astype(jnp.int32)
     copy = pltpu.make_async_copy(keys_vmem, keys_smem, sem)
     copy.start()
@@ -85,44 +103,65 @@
 
     @pl.loop(0, NSRC // 4)
     def _(i):
-        for s in range(4):
-            source = i * 4 + s
-            for pair in range((NT + 1) // 2):
-                start = pl.multiple_of(source * UNIT + pair * 2 * SUB, 2 * SUB)
-                two = in_ref[pl.ds(start, 2 * SUB), :].astype(jnp.float32)
-                for half in range(2):
-                    t = pair * 2 + half
+        for d in range(2):
+            for pair in range(tiles):
+                start = pl.multiple_of((i * 2 + d) * DUO + pair * PAIR, PAIR)
+                two = in_ref[pl.ds(start, PAIR), :].astype(jnp.float32)
+                for part in range(2):
+                    which, place = divmod(pair * 2 + part, tiles)
+                    t, half = divmod(place, 2)
                     if t < NT:
-                        acc = accs[(s * NT + t) % NACC]
-                        where = pl.ds(pl.multiple_of(keys_smem[source, t] * SUB, SUB), SUB)
-                        acc[where, :] = acc[where, :] + two[half * SUB : (half + 1) * SUB]
-
-    total = accs[0][...]
-    for acc in accs[1:]:
-        total = total + acc[...]
-    total = total.astype(jnp.bfloat16)
-    for x in range(4):
-        out_ref[x] = total
-
-
-def make_sums(arrived):
+                        acc = accs[half * COPIES + (which + t) % COPIES]
+                        row = keys_smem[i * 4 + d * 2 + which, t] * SUB
+                        where = pl.ds(pl.multiple_of(row, SUB), SUB)
+                        acc[where, :] = acc[where, :] + two[part * SUB : (part + 1) * SUB]
+
+    left = accs[0][...] + accs[1][...]
+    right = accs[2][...] + accs[3][...]
+    first_core = core_ref[0] == 0
+    keep_ref[...] = jnp.where(first_core, left, right)
+    send_ref[...] = jnp.where(first_core, right, left)
+
+
+def make_sums(core, arrived):
+    half = jax.ShapeDtypeStruct((BUCKETS * SUB, LANES), jnp.float32)
     return pl.pallas_call(
         sum_kernel,
-        in_specs=[pl.BlockSpec(memory_space=pltpu.VMEM)],
-        out_specs=pl.BlockSpec(memory_space=pltpu.VMEM),
-        out_shape=jax.ShapeDtypeStruct((4, BUCKETS * SUB, LANES), jnp.bfloat16),
+        in_specs=[
+            pl.BlockSpec(memory_space=pltpu.SMEM),
+            pl.BlockSpec(memory_space=pltpu.VMEM),
+        ],
+        out_specs=[pl.BlockSpec(memory_space=pltpu.VMEM)] * 2,
+        out_shape=[half, half],
         scratch_shapes=[
             pltpu.VMEM((NSRC, LANES), jnp.int32),
             pltpu.SMEM((NSRC, LANES), jnp.int32),
             pltpu.SemaphoreType.DMA,
         ]
-        + [pltpu.VMEM((BUCKETS * SUB, LANES), jnp.float32)] * NACC,
+        + [pltpu.VMEM((BUCKETS * SUB, LANES), jnp.float32)] * (2 * COPIES),
         compiler_params=pltpu.CompilerParams(vmem_limit_bytes=32 * MIB),
         cost_estimate=pl.CostEstimate(
-            flops=NSRC * NT * BLK, bytes_accessed=2 * MIB, transcendentals=0
+            flops=NSRC * NT * 2 * BLK, bytes_accessed=2 * MIB, transcendentals=0
         ),
         name="sums",
-    )(arrived)
+    )(core, arrived)
+
+
+def join_kernel(keep_ref, got_ref, out_ref):
+    total = (keep_ref[...] + got_ref[...]).astype(jnp.bfloat16)
+    for x in range(4):
+        out_ref[x] = total
+
+
+def make_join(keep, got):
+    return pl.pallas_call(
+        join_kernel,
+        in_specs=[pl.BlockSpec(memory_space=pltpu.VMEM)] * 2,
+        out_specs=pl.BlockSpec(memory_space=pltpu.VMEM),
+        out_shape=jax.ShapeDtypeStruct((4, BUCKETS * SUB, LANES), jnp.bfloat16),
+        compiler_params=pltpu.CompilerParams(vmem_limit_bytes=32 * MIB),
+        name="join",
+    )(keep, got)
 
 
 HALF = LANES // 2
@@ -175,8 +214,10 @@
     pieces = make_pieces(
         three_center, pair_mu[0], pair_site[0, :, 0], pair_pos[0], row.reshape(1), coeff
     )
-    arrived = lax.all_to_all(pieces, ALL_MU, split_axis=0, concat_axis=0, tiled=True)
-    sums = make_sums(arrived)
+    arrived = lax.all_to_all(pieces, MAIN, split_axis=0, concat_axis=0, tiled=True)
+    keep, send = make_sums(lax.axis_index("c").reshape(1), arrived)
+    got = lax.ppermute(send, "c", [(0, 1), (1, 0)])
+    sums = make_join(keep, got)
     gathered = lax.all_to_all(
         sums.reshape(16, NU_SITE * SUB, LANES), FIT, split_axis=0, concat_axis=0, tiled=True
     )

time: 86.9 us -> 82.4 us (0.948)
  blocking collectives: 59.7 us -> 0 us
  waiting for transfers between devices: 8.39 us -> 43.7 us
  starting transfers between devices: 6.12 us -> 28.8 us
  local copies, waits for them, and re-layouts: 4.63 us -> 0.01 us
  Pallas kernels: 7.77 us -> 9.54 us
    all_to_all x1 -> x0, blocking collectives: 59.7 us -> none  [local(): lax.all_to_all(pieces, ALL_MU, split_axis=0, concat_axis=0, tiled=True)]
    all_to_all x0 -> x1, waiting for transfers between devices: none -> 34.3 us  [local(): lax.all_to_all(pieces, MAIN, split_axis=0, concat_axis=0, tiled=True)]
    all_to_all x0 -> x1, starting transfers between devices: none -> 17.1 us  [local(): lax.all_to_all(pieces, MAIN, split_axis=0, concat_axis=0, tiled=True)]
    ppermute x0 -> x1, starting transfers between devices: none -> 6.34 us  [local(): got = lax.ppermute(send, 'c', [(0, 1), (1, 0)])]
    unnamed x12 -> x2, local copies, waits for them, and re-layouts: 4.63 us -> 0.01 us
    pallas_call x1, Pallas kernels: 2.94 us -> 5.48 us  [make_pieces(): pl.pallas_call(piece_kernel, grid_spec=pltpu.PrefetchScalarGridSpec(num_s...]
    ppermute x0 -> x1, waiting for transfers between devices: none -> 1.05 us  [local(): got = lax.ppermute(send, 'c', [(0, 1), (1, 0)])]
    pallas_call x1 -> x2, Pallas kernels: 3.77 us -> 3.01 us  [the longest x1 2.23 us: make_sums(): pl.pallas_call(sum_kernel, in_specs=[pl.BlockSpec(memory_space=pltpu.SMEM...]
  transfers between devices with their start and end apart: 1 -> 3, of which waited for: 1 -> 3; matrix products, arithmetic and copies ran while one was open for 0% -> 0% of each run, Pallas kernels for 0% -> 0%
where the time goes in v3:
time: 82.4 us; the launch traced here: 82 us
  waiting for transfers between devices  43.7 us (53%)
  starting transfers between devices  28.8 us (35%)
  Pallas kernels  9.54 us (12%)
    all_to_all x1, waiting for transfers between devices, local(): lax.all_to_all(pieces, MAIN, split_axis=0, concat_axis=0, tiled=True)  34.3 us
    all_to_all x1, starting transfers between devices, local(): lax.all_to_all(pieces, MAIN, split_axis=0, concat_axis=0, tiled=True)  17.1 us
    all_to_all x1, waiting for transfers between devices, local(): lax.all_to_all(sums.reshape(16, NU_SITE * SUB, LANES), FIT, split_axis=0,...  8.39 us
    ppermute x1, starting transfers between devices, local(): got = lax.ppermute(send, 'c', [(0, 1), (1, 0)])  6.34 us
    pallas_call x1, Pallas kernels, make_pieces(): pl.pallas_call(piece_kernel, grid_spec=pltpu.PrefetchScalarGridSpec(num_s...  5.48 us
    all_to_all x1, starting transfers between devices, local(): lax.all_to_all(sums.reshape(16, NU_SITE * SUB, LANES), FIT, split_axis=0,...  5.28 us
    pallas_call x1, Pallas kernels, make_sums(): pl.pallas_call(sum_kernel, in_specs=[pl.BlockSpec(memory_space=pltpu.SMEM...  2.23 us
  transfers between devices with their start and end apart: 3, of which 3 were waited for; matrix products, arithmetic and copies ran while one was open for 0% of the time, Pallas kernels for 0%

profile of v3, /device:TPU:1, one launch (start us, length us, event | category | flops | bytes accessed | tf_op | source)
XLA Modules:
  0.0 82.0 jit_solution(16467550633137794298)
XLA Ops:
  0.0 5.5 %pieces.1 = bf16[5632,128]{1,0:T(8,128)(2,1)} custom-call(s32[5]{0:T(128)} %bitcast.20, s32[5]{0:T(128)} %bitcast.21, s32[5]{0:T(128)} %bitcast.22, s32[1]{0:T(128)} %bitcast.5.row_ref, bf16[5,64,4096]{2,1,0:T(8,128)(2,1)} %slab_ref.1, bf16[32,3072]{1,0:T(8,128)(2,1)} %bitcast.15, bf16[32,3072]{1,0:T(8,128)(2,1)} %bitcast.16, bf16[32,3072]{1,0:T(8,128)(2,1)} %bitcast.17, ...), custom_call_target="tpu_custom_call" | custom-call | flops 83886080 | bytes 4194304 | tf_op jit(solution)/shard_map/pieces/pallas_call | solution.py:65
  5.5 17.1 %all-to-all-start = ((bf16[64,88,128]{2,1,0:T(8,128)(2,1)}), bf16[64,88,128]{2,1,0:T(8,128)(2,1)S(1)}, u32[]{:S(2)}, u32[]{:S(2)}) async-start(bf16[64,88,128]{2,1,0:T(8,128)(2,1)} %bitcast.14), calls=%async_computation | async-start | bytes 2883584 | tf_op jit(solution)/shard_map/all_to_all | solution.py:217
  22.6 0.0 copy-start
  22.6 34.3 %all-to-all-done = bf16[64,88,128]{2,1,0:T(8,128)(2,1)S(1)} async-done(((bf16[64,88,128]{2,1,0:T(8,128)(2,1)}), bf16[64,88,128]{2,1,0:T(8,128)(2,1)S(1)}, u32[]{:S(2)}, u32[]{:S(2)}) %all-to-all-start) | async-done | bytes 1441824 | tf_op jit(solution)/shard_map/all_to_all | solution.py:217
  56.9 2.2 %sums.1 = (f32[384,128]{1,0:T(8,128)S(1)}, f32[384,128]{1,0:T(8,128)S(1)}) custom-call(s32[1]{0:T(128)} %bitcast.1.core_ref, bf16[5632,128]{1,0:T(8,128)(2,1)S(1)} %bitcast.12), custom_call_target="tpu_custom_call" | custom-call | flops 655360 | bytes 2097152 | tf_op jit(solution)/shard_map/sums/pallas_call | solution.py:128
  59.1 6.3 %collective-permute-start = (f32[384,128]{1,0:T(8,128)S(1)}, f32[384,128]{1,0:T(8,128)S(1)}, u32[]{:S(2)}, u32[]{:S(2)}) collective-permute-start(f32[384,128]{1,0:T(8,128)S(1)} %get-tuple-element.8), channel_id=1, source_target_pairs={{0,4},{4,0},{1,5},{5,1},{2,6},{6,2},{3,7},{7,3},{8,12},{12,8},{9,1... | collective-permute-start | bytes 589832 | tf_op jit(solution)/shard_map/ppermute | solution.py:219
  65.5 1.0 %collective-permute-done.got_ref = f32[384,128]{1,0:T(8,128)S(1)} collective-permute-done((f32[384,128]{1,0:T(8,128)S(1)}, f32[384,128]{1,0:T(8,128)S(1)}, u32[]{:S(2)}, u32[]{:S(2)}) %collective-permute-start) | collective-permute-done | bytes 196640 | tf_op jit(solution)/shard_map/ppermute | solution.py:219
  66.5 0.8 join.1
  67.3 5.3 %all-to-all-start.1 = ((bf16[16,96,128]{2,1,0:T(8,128)(2,1)}), bf16[16,96,128]{2,1,0:T(8,128)(2,1)S(1)}, u32[]{:S(2)}, u32[]{:S(2)}) async-start(bf16[16,96,128]{2,1,0:T(8,128)(2,1)} %bitcast.9), calls=%async_computation.1 | async-start | bytes 786432 | tf_op jit(solution)/shard_map/all_to_all | solution.py:221
  72.6 8.4 %all-to-all-done.1 = bf16[16,96,128]{2,1,0:T(8,128)(2,1)S(1)} async-done(((bf16[16,96,128]{2,1,0:T(8,128)(2,1)}), bf16[16,96,128]{2,1,0:T(8,128)(2,1)S(1)}, u32[]{:S(2)}, u32[]{:S(2)}) %all-to-all-start.1) | async-done | bytes 393248 | tf_op jit(solution)/shard_map/all_to_all | solution.py:221
  81.0 0.0 copy-done
  81.0 1.1 %fit.1 = bf16[12,4096]{1,0:T(8,128)(2,1)} custom-call(s32[1]{0:T(128)} %bitcast.site_ref, bf16[4,4,96,128]{3,2,1,0:T(8,128)(2,1)S(1)} %bitcast.13, bf16[48,64,256]{2,1,0:T(8,128)(2,1)S(1)} %copy-done), custom_call_target="tpu_custom_call" | custom-call | tf_op jit(solution)/shard_map/fit/pallas_call | solution.py:194
Async XLA Ops:
  5.5 51.4 %all-to-all-start = ((bf16[64,88,128]{2,1,0:T(8,128)(2,1)}), bf16[64,88,128]{2,1,0:T(8,128)(2,1)S(1)}, u32[]{:S(2)}, u32[]{:S(2)}) async-start(bf16[64,88,128]{2,1,0:T(8,128)(2,1)} %bitcast.14), calls=%async_computation | async-start | bytes 2883584 | tf_op jit(solution)/shard_map/all_to_all | solution.py:217
  22.6 58.4 %copy-start = (bf16[48,64,256]{2,1,0:T(8,128)(2,1)S(1)}, bf16[48,64,256]{2,1,0:T(8,128)(2,1)}, u32[]{:S(2)}) copy-start(bf16[48,64,256]{2,1,0:T(8,128)(2,1)} %weight_ref.1) | copy-start | bytes 4718596
  59.1 7.4 %collective-permute-start = (f32[384,128]{1,0:T(8,128)S(1)}, f32[384,128]{1,0:T(8,128)S(1)}, u32[]{:S(2)}, u32[]{:S(2)}) collective-permute-start(f32[384,128]{1,0:T(8,128)S(1)} %get-tuple-element.8), channel_id=1, source_target_pairs={{0,4},{4,0},{1,5},{5,1},{2,6},{6,2},{3,7},{7,3},{8,12},{12,8},{9,1... | collective-permute-start | bytes 589832 | tf_op jit(solution)/shard_map/ppermute | solution.py:219
  67.3 13.7 %all-to-all-start.1 = ((bf16[16,96,128]{2,1,0:T(8,128)(2,1)}), bf16[16,96,128]{2,1,0:T(8,128)(2,1)S(1)}, u32[]{:S(2)}, u32[]{:S(2)}) async-start(bf16[16,96,128]{2,1,0:T(8,128)(2,1)} %bitcast.9), calls=%async_computation.1 | async-start | bytes 786432 | tf_op jit(solution)/shard_map/all_to_all | solution.py:221

commit v4 on v2

v4 whole, which is shorter than its diff:
```python
import jax
import jax.numpy as jnp
from jax import lax
from jax.experimental import pallas as pl
from jax.experimental.pallas import tpu as pltpu
from jax.sharding import Mesh, PartitionSpec as P

SITES = 4
NU_SITE = 12
NT = 5
BS = 64
NOB = 32
LANES = 128
NSRC = 128
BUCKETS = SITES * NU_SITE
BLK = 1024
SUB = BLK // LANES
UNIT = NT * SUB
ALL_MU = ("yl", "c", "zh", "zl", "yh")
FIT = ("x", "yl", "c")
MIB = 2**20


def piece_kernel(mu_hbm, slab_hbm, coeff_hbm, out_hbm, mu, slab, coeff, scr, done, small, ins, outs):
    def slab_copy(q):
        return pltpu.make_async_copy(
            slab_hbm.at[:, :, pl.ds(q * BLK, BLK)], slab.at[q], ins.at[q]
        )

    def out_copy(q):
        rows = pl.ds(q * NOB * UNIT, NOB * UNIT)
        return pltpu.make_async_copy(done.at[q], out_hbm.at[rows, :], outs.at[q])

    mu_copy = pltpu.make_async_copy(mu_hbm, mu, small.at[0])
    coeff_copy = pltpu.make_async_copy(coeff_hbm, coeff, small.at[1])
    mu_copy.start()
    coeff_copy.start()
    for q in range(SITES):
        slab_copy(q).start()
    mu_copy.wait()
    coeff_copy.wait()
    mine = []
    for t in range(NT):
        block = mu[0, t]
        both = coeff[:, pl.ds(pl.multiple_of(block // 2 * LANES, LANES), LANES)].astype(jnp.float32)
        mine.append(
            jnp.where(block % 2 == 1, both[:, BS:], both[:, :BS]).astype(jnp.bfloat16)
        )
    for q in range(SITES):
        slab_copy(q).wait()
        for t in range(NT):
            res = jnp.dot(mine[t], slab[q, t], preferred_element_type=jnp.float32)
            for j in range(SUB):
                scr[pl.ds(t * SUB + j, NOB, stride=UNIT), :] = res[
                    :, j * LANES : (j + 1) * LANES
                ]
        done[q] = scr[...].astype(jnp.bfloat16)
        out_copy(q).start()
    for q in range(SITES):
        out_copy(q).wait()


def make_pieces(three_center, pair_mu, coeff):
    return pl.pallas_call(
        piece_kernel,
        in_specs=[pl.BlockSpec(memory_space=pl.ANY)] * 3,
        out_specs=pl.BlockSpec(memory_space=pl.ANY),
        out_shape=jax.ShapeDtypeStruct((SITES * NOB * UNIT, LANES), jnp.bfloat16),
        scratch_shapes=[
            pltpu.SMEM((1, NT), jnp.int32),
            pltpu.VMEM((SITES, NT, BS, BLK), jnp.bfloat16),
            pltpu.VMEM((NOB, 3072), jnp.bfloat16),
            pltpu.VMEM((NOB * UNIT, LANES), jnp.float32),
            pltpu.VMEM((SITES, NOB * UNIT, LANES), jnp.bfloat16),
            pltpu.SemaphoreType.DMA((2,)),
            pltpu.SemaphoreType.DMA((SITES,)),
            pltpu.SemaphoreType.DMA((SITES,)),
        ],
        compiler_params=pltpu.CompilerParams(vmem_limit_bytes=58 * MIB),
        cost_estimate=pl.CostEstimate(
            flops=2 * NT * BS * NOB * 4096, bytes_accessed=4 * MIB, transcendentals=0
        ),
        name="pieces",
    )(pair_mu, three_center, coeff.T)


NACC = 4


def sum_kernel(key_ref, in_ref, out_ref, *accs):
    for acc in accs:
        acc[...] = jnp.zeros_like(acc)

    @pl.loop(0, NSRC // 4)
    def _(i):
        for pair in range(2 * NT):
            start = pl.multiple_of(i * 4 * UNIT + pair * 2 * SUB, 2 * SUB)
            two = in_ref[pl.ds(start, 2 * SUB), :].astype(jnp.float32)
            for half in range(2):
                which, t = divmod(pair * 2 + half, NT)
                acc = accs[(pair * 2 + half) % NACC]
                where = pl.ds(pl.multiple_of(key_ref[i * 4 + which, t] * SUB, SUB), SUB)
                acc[where, :] = acc[where, :] + two[half * SUB : (half + 1) * SUB]

    total = accs[0][...]
    for acc in accs[1:]:
        total = total + acc[...]
    total = total.astype(jnp.bfloat16)
    for x in range(4):
        out_ref[x] = total


def make_sums(keys, arrived):
    return pl.pallas_call(
        sum_kernel,
        in_specs=[
            pl.BlockSpec(memory_space=pltpu.SMEM),
            pl.BlockSpec(memory_space=pltpu.VMEM),
        ],
        out_specs=pl.BlockSpec(memory_space=pltpu.VMEM),
        out_shape=jax.ShapeDtypeStruct((4, BUCKETS * SUB, LANES), jnp.bfloat16),
        scratch_shapes=[pltpu.VMEM((BUCKETS * SUB, LANES), jnp.float32)] * NACC,
        compiler_params=pltpu.CompilerParams(vmem_limit_bytes=32 * MIB),
        cost_estimate=pl.CostEstimate(
            flops=NSRC * NT * BLK, bytes_accessed=2 * MIB, transcendentals=0
        ),
        name="sums",
    )(keys, arrived)


HALF = LANES // 2
NHI = 32
KPAD = 16


def fit_kernel(site_ref, in_ref, weight_ref, out_ref, scr):
    for k in range(NU_SITE):
        rows = [
            jnp.concatenate([in_ref[x, q, pl.ds(k * SUB, SUB), :] for q in range(4)], axis=0)
            for x in range(4)
        ]
        low = jnp.concatenate([r[:, :HALF] for r in rows], axis=1)
        high = jnp.concatenate([r[:, HALF:] for r in rows], axis=1)
        res = lax.dot_general(
            jnp.concatenate([low, high], axis=0),
            weight_ref[k],
            (((1,), (1,)), ((), ())),
            preferred_element_type=jnp.float32,
        )
        scr[pl.ds(k, NHI, stride=KPAD), :] = jnp.concatenate([res[:NHI], res[NHI:]], axis=1)
    for n in range(NHI):
        out_ref[:, n * LANES : (n + 1) * LANES] = scr[n * KPAD : n * KPAD + NU_SITE, :].astype(
            jnp.bfloat16
        )


def make_fit(site, gathered, fitting):
    return pl.pallas_call(
        fit_kernel,
        grid_spec=pltpu.PrefetchScalarGridSpec(
            num_scalar_prefetch=1,
            grid=(1,),
            in_specs=[
                pl.BlockSpec((4, 4, NU_SITE * SUB, LANES), lambda i, site: (0, 0, 0, 0)),
                pl.BlockSpec((NU_SITE, 64, 256), lambda i, site: (site[0], 0, 0)),
            ],
            out_specs=pl.BlockSpec((NU_SITE, NHI * LANES), lambda i, site: (0, 0)),
            scratch_shapes=[pltpu.VMEM((NHI * KPAD, LANES), jnp.float32)],
        ),
        out_shape=jax.ShapeDtypeStruct((NU_SITE, NHI * LANES), jnp.bfloat16),
        compiler_params=pltpu.CompilerParams(vmem_limit_bytes=32 * MIB),
        name="fit",
    )(site, gathered, fitting)


def local(three_center, pair_mu, pair_site, pair_pos, coeff, fitting):
    pieces = make_pieces(three_center, pair_mu, coeff)
    keys = jnp.pad(pair_site[:, :, 0] * NU_SITE + pair_pos, ((0, 0), (0, LANES - NT)))
    for axis in reversed(ALL_MU):
        keys = lax.all_gather(keys, axis, axis=0, tiled=True)
    arrived = lax.all_to_all(pieces, ALL_MU, split_axis=0, concat_axis=0, tiled=True)
    sums = make_sums(keys, arrived)
    gathered = lax.all_to_all(
        sums.reshape(16, NU_SITE * SUB, LANES), FIT, split_axis=0, concat_axis=0, tiled=True
    )
    site = lax.axis_index("yl") * 2 + lax.axis_index("c")
    result = make_fit(site.reshape(1), gathered.reshape(4, 4, NU_SITE * SUB, LANES), fitting)
    return result.reshape(1, NU_SITE, 1, 4096)


def solution(mesh):
    fine = Mesh(mesh.devices.reshape(4, 2, 4, 2, 2, 4), ("zh", "zl", "yh", "yl", "c", "x"))
    mu = ("zh", "zl", "yh", "yl", "c")
    in_specs = (
        P(mu, None, "x"),
        P(mu, None),
        P(mu, None, None),
        P(mu, None),
        P(),
        P(None, "x", None),
    )
    out_specs = P(mu, None, None, "x")
    return jax.shard_map(local, mesh=fine, in_specs=in_specs, out_specs=out_specs, check_vma=False)
```

time: 86.9 us -> 102 us (1.17)
  starting transfers between devices: 6.12 us -> 24.4 us
  local copies, waits for them, and re-layouts: 4.63 us -> 0.02 us
    all_gather x0 -> x5, blocking collectives: none -> 60.7 us  [local(): keys = lax.all_gather(keys, axis, axis=0, tiled=True)]
    all_to_all x1 -> x0, blocking collectives: 59.7 us -> none  [local(): lax.all_to_all(pieces, ALL_MU, split_axis=0, concat_axis=0, tiled=True)]
    all_to_all x0 -> x1, starting transfers between devices: none -> 18.5 us  [local(): lax.all_to_all(pieces, ALL_MU, split_axis=0, concat_axis=0, tiled=True)]
    unnamed x12 -> x7, local copies, waits for them, and re-layouts: 4.63 us -> 0.02 us
  transfers between devices with their start and end apart: 1 -> 2, of which waited for: 1 -> 1; matrix products, arithmetic and copies ran while one was open for 0% -> 0% of each run, Pallas kernels for 0% -> 0%
where the time goes in v4:
time: 102 us
  blocking collectives  60.7 us (60%)
  starting transfers between devices  24.4 us (24%)
  waiting for transfers between devices  8.39 us (8%)
  Pallas kernels  8.23 us (8%)
    all_gather x5, blocking collectives, local(): keys = lax.all_gather(keys, axis, axis=0, tiled=True)  60.7 us
    all_to_all x1, starting transfers between devices, local(): lax.all_to_all(pieces, ALL_MU, split_axis=0, concat_axis=0, tiled=True)  18.5 us
    all_to_all x1, waiting for transfers between devices, local(): lax.all_to_all(sums.reshape(16, NU_SITE * SUB, LANES), FIT, split_axis=0,...  8.39 us
    all_to_all x1, starting transfers between devices, local(): lax.all_to_all(sums.reshape(16, NU_SITE * SUB, LANES), FIT, split_axis=0,...  5.86 us
    pallas_call x1, Pallas kernels, make_sums(): pl.pallas_call(sum_kernel, in_specs=[pl.BlockSpec(memory_space=pltpu.SMEM...  3.62 us
    pallas_call x1, Pallas kernels, make_pieces(): pl.pallas_call(piece_kernel, in_specs=[pl.BlockSpec(memory_space=pl.ANY)]...  3.55 us
  transfers between devices with their start and end apart: 2, of which 1 were waited for; matrix products, arithmetic and copies ran while one was open for 0% of the time, Pallas kernels for 0%

profile of v4, /device:TPU:1, one launch (start us, length us, event | category | flops | bytes accessed | tf_op | source)
XLA Modules:
  0.0 101.9 jit_solution(17286612853803784517)
XLA Ops:
  0.0 3.6 %pieces.1 = bf16[5120,128]{1,0:T(8,128)(2,1)} custom-call(s32[1,5]{1,0:T(1,128)} %mu_hbm.1, bf16[5,64,4096]{2,1,0:T(8,128)(2,1)} %slab_hbm.1, bf16[32,3072]{1,0:T(8,128)(2,1)} %bitcast.16), custom_call_target="tpu_custom_call" | custom-call | flops 83886080 | bytes 4194304 | tf_op jit(solution)/shard_map/pieces/pallas_call | solution.py:64
  3.6 0.0 copy-start.1
  3.6 0.0 copy-start.2
  3.6 18.5 %all-to-all-start = ((bf16[128,40,128]{2,1,0:T(8,128)(2,1)}), bf16[128,40,128]{2,1,0:T(8,128)(2,1)S(1)}, u32[]{:S(2)}, u32[]{:S(2)}) async-start(bf16[128,40,128]{2,1,0:T(8,128)(2,1)} %bitcast.15), calls=%async_computation | async-start | bytes 2621440 | tf_op jit(solution)/shard_map/all_to_all | solution.py:181
  22.1 0.0 copy-done.1
  22.1 0.0 copy-done.2
  22.1 0.0 copy-start
  22.2 34.4 %all-gather = s32[4,1,128]{2,1,0:T(1,128)S(1)} all-gather(s32[1,1,128]{2,1,0:T(1,128)S(1)} %pad_bitcast_fusion), channel_id=1, replica_groups=mesh['zh'=4,'zl'=2,'yh'=4,'yl'=2,'c'=2,'x'=4] {'yh'}, dimensions={0}, use_global_device_ids=true | all-gather | bytes 2560 | tf_op jit(solution)/shard_map/all_gather | solution.py:180
  56.6 3.2 %all-gather.1 = s32[2,4,128]{2,1,0:T(4,128)S(1)} all-gather(s32[1,4,128]{2,1,0:T(4,128)S(1)} %bitcast.18), channel_id=1, replica_groups=mesh['zh'=4,'zl'=2,'yh'=4,'yl'=2,'c'=2,'x'=4] {'zl'}, dimensions={0}, use_global_device_ids=true | all-gather | bytes 6144 | tf_op jit(solution)/shard_map/all_gather | solution.py:180
  59.8 12.4 %all_gather.17 = s32[32,128]{1,0:T(8,128)S(1)} all-gather(s32[8,128]{1,0:T(8,128)S(1)} %bitcast.17), channel_id=1, replica_groups=mesh['zh'=4,'zl'=2,'yh'=4,'yl'=2,'c'=2,'x'=4] {'zh'}, dimensions={0}, use_global_device_ids=true | all-gather | bytes 20480 | tf_op jit(solution)/shard_map/all_gather | solution.py:180
  72.2 7.3 %all_gather.18 = s32[64,128]{1,0:T(8,128)S(1)} all-gather(s32[32,128]{1,0:T(8,128)S(1)} %all_gather.17), channel_id=1, replica_groups=mesh['zh'=4,'zl'=2,'yh'=4,'yl'=2,'c'=2,'x'=4] {'c'}, dimensions={0}, use_global_device_ids=true | all-gather | bytes 49152 | tf_op jit(solution)/shard_map/all_gather | solution.py:180
  79.5 3.4 %all_gather.19.key_ref = s32[128,128]{1,0:T(8,128)S(1)} all-gather(s32[64,128]{1,0:T(8,128)S(1)} %all_gather.18), channel_id=1, replica_groups=mesh['zh'=4,'zl'=2,'yh'=4,'yl'=2,'c'=2,'x'=4] {'yl'}, dimensions={0}, use_global_device_ids=true | all-gather | bytes 98304 | tf_op jit(solution)/shard_map/all_gather | solution.py:180
  82.9 0.0 all-to-all-done
  82.9 3.6 %sums.1 = bf16[4,384,128]{2,1,0:T(8,128)(2,1)} custom-call(s32[128,128]{1,0:T(8,128)S(1)} %all_gather.19.key_ref, bf16[5120,128]{1,0:T(8,128)(2,1)S(1)} %bitcast.13), custom_call_target="tpu_custom_call" | custom-call | flops 655360 | bytes 2097152 | tf_op jit(solution)/shard_map/sums/pallas_call | solution.py:114
  86.6 5.9 %all-to-all-start.1 = ((bf16[16,96,128]{2,1,0:T(8,128)(2,1)}), bf16[16,96,128]{2,1,0:T(8,128)(2,1)S(1)}, u32[]{:S(2)}, u32[]{:S(2)}) async-start(bf16[16,96,128]{2,1,0:T(8,128)(2,1)} %bitcast.8), calls=%async_computation.1 | async-start | bytes 786432 | tf_op jit(solution)/shard_map/all_to_all | solution.py:183
  92.4 8.4 %all-to-all-done.1 = bf16[16,96,128]{2,1,0:T(8,128)(2,1)S(1)} async-done(((bf16[16,96,128]{2,1,0:T(8,128)(2,1)}), bf16[16,96,128]{2,1,0:T(8,128)(2,1)S(1)}, u32[]{:S(2)}, u32[]{:S(2)}) %all-to-all-start.1) | async-done | bytes 393248 | tf_op jit(solution)/shard_map/all_to_all | solution.py:183
  100.8 0.0 copy-done
  100.8 1.1 %fit.1 = bf16[12,4096]{1,0:T(8,128)(2,1)} custom-call(s32[1]{0:T(128)} %bitcast.site_ref, bf16[4,4,96,128]{3,2,1,0:T(8,128)(2,1)S(1)} %bitcast.14, bf16[48,64,256]{2,1,0:T(8,128)(2,1)S(1)} %copy-done), custom_call_target="tpu_custom_call" | custom-call | tf_op jit(solution)/shard_map/fit/pallas_call | solution.py:158
  (2 shorter events, 0.0 us)
Async XLA Ops:
  3.6 18.6 %copy-start.1 = (s32[1,5]{1,0:T(1,128)S(1)}, s32[1,5]{1,0:T(1,128)}, u32[]{:S(2)}) copy-start(s32[1,5]{1,0:T(1,128)} %param.9) | copy-start | bytes 64
  3.6 18.6 %copy-start.2 = (s32[1,5,1]{1,2,0:T(1,128)S(1)}, s32[1,5,1]{1,2,0:T(1,128)}, u32[]{:S(2)}) copy-start(s32[1,5,1]{1,2,0:T(1,128)} %param.8) | copy-start | bytes 64
  3.6 79.3 %all-to-all-start = ((bf16[128,40,128]{2,1,0:T(8,128)(2,1)}), bf16[128,40,128]{2,1,0:T(8,128)(2,1)S(1)}, u32[]{:S(2)}, u32[]{:S(2)}) async-start(bf16[128,40,128]{2,1,0:T(8,128)(2,1)} %bitcast.15), calls=%async_computation | async-start | bytes 2621440 | tf_op jit(solution)/shard_map/all_to_all | solution.py:181
  22.1 78.7 %copy-start = (bf16[48,64,256]{2,1,0:T(8,128)(2,1)S(1)}, bf16[48,64,256]{2,1,0:T(8,128)(2,1)}, u32[]{:S(2)}) copy-start(bf16[48,64,256]{2,1,0:T(8,128)(2,1)} %weight_ref.1) | copy-start | bytes 4718596
  86.6 14.2 %all-to-all-start.1 = ((bf16[16,96,128]{2,1,0:T(8,128)(2,1)}), bf16[16,96,128]{2,1,0:T(8,128)(2,1)S(1)}, u32[]{:S(2)}, u32[]{:S(2)}) async-start(bf16[16,96,128]{2,1,0:T(8,128)(2,1)} %bitcast.8), calls=%async_computation.1 | async-start | bytes 786432 | tf_op jit(solution)/shard_map/all_to_all | solution.py:183

commit v5 on v4

--- a/solution.py
+++ b/solution.py
@@ -15,13 +15,22 @@
 BUCKETS = SITES * NU_SITE
 BLK = 1024
 SUB = BLK // LANES
-UNIT = NT * SUB
-ALL_MU = ("yl", "c", "zh", "zl", "yh")
+DATA = NT * SUB
+UNIT = DATA + 2
+ALL_MU = ("yl", "c", "z", "yh")
 FIT = ("x", "yl", "c")
 MIB = 2**20
 
 
-def piece_kernel(mu_hbm, slab_hbm, coeff_hbm, out_hbm, mu, slab, coeff, scr, done, small, ins, outs):
+def source_index():
+    quarter = lax.axis_index("yl") * 2 + lax.axis_index("c")
+    return (quarter * 8 + lax.axis_index("z")) * 4 + lax.axis_index("yh")
+
+
+def piece_kernel(
+    mu_hbm, site_hbm, pos_hbm, slab_hbm, coeff_hbm, out_hbm,
+    mu, site, pos, slab, coeff, scr, done, small, ins, outs,
+):
     def slab_copy(q):
         return pltpu.make_async_copy(
             slab_hbm.at[:, :, pl.ds(q * BLK, BLK)], slab.at[q], ins.at[q]
@@ -31,14 +40,27 @@
         rows = pl.ds(q * NOB * UNIT, NOB * UNIT)
         return pltpu.make_async_copy(done.at[q], out_hbm.at[rows, :], outs.at[q])
 
-    mu_copy = pltpu.make_async_copy(mu_hbm, mu, small.at[0])
-    coeff_copy = pltpu.make_async_copy(coeff_hbm, coeff, small.at[1])
-    mu_copy.start()
-    coeff_copy.start()
+    smalls = [
+        pltpu.make_async_copy(src, dst, small.at[i])
+        for i, (src, dst) in enumerate(
+            [(mu_hbm, mu), (coeff_hbm, coeff), (site_hbm, site), (pos_hbm, pos)]
+        )
+    ]
+    for copy in smalls:
+        copy.start()
     for q in range(SITES):
         slab_copy(q).start()
-    mu_copy.wait()
-    coeff_copy.wait()
+    me = source_index()
+    shift = me % 4 * 2
+    first_lane = me // 8 * 8
+    for copy in smalls:
+        copy.wait()
+    lane = lax.broadcasted_iota(jnp.int32, (NOB, LANES), 1)
+    keys = jnp.zeros((NOB, LANES), jnp.int32)
+    for t in range(NT):
+        keys = jnp.where(lane == first_lane + t, site[0, t] * NU_SITE + pos[0, t], keys)
+    for r in range(2):
+        scr[pl.ds(DATA + r, NOB, stride=UNIT), :] = keys.astype(jnp.float32)
     mine = []
     for t in range(NT):
         block = mu[0, t]
@@ -51,7 +73,9 @@
         for t in range(NT):
             res = jnp.dot(mine[t], slab[q, t], preferred_element_type=jnp.float32)
             for j in range(SUB):
-                scr[pl.ds(t * SUB + j, NOB, stride=UNIT), :] = res[
+                place = t * SUB + j - shift
+                place = jnp.where(place < 0, place + DATA, place)
+                scr[pl.ds(place, NOB, stride=UNIT), :] = res[
                     :, j * LANES : (j + 1) * LANES
                 ]
         done[q] = scr[...].astype(jnp.bfloat16)
@@ -60,19 +84,21 @@
         out_copy(q).wait()
 
 
-def make_pieces(three_center, pair_mu, coeff):
+def make_pieces(three_center, pair_mu, pair_site, pair_pos, coeff):
     return pl.pallas_call(
         piece_kernel,
-        in_specs=[pl.BlockSpec(memory_space=pl.ANY)] * 3,
+        in_specs=[pl.BlockSpec(memory_space=pl.ANY)] * 5,
         out_specs=pl.BlockSpec(memory_space=pl.ANY),
         out_shape=jax.ShapeDtypeStruct((SITES * NOB * UNIT, LANES), jnp.bfloat16),
         scratch_shapes=[
+            pltpu.SMEM((1, NT), jnp.int32),
+            pltpu.SMEM((1, NT), jnp.int32),
             pltpu.SMEM((1, NT), jnp.int32),
             pltpu.VMEM((SITES, NT, BS, BLK), jnp.bfloat16),
             pltpu.VMEM((NOB, 3072), jnp.bfloat16),
             pltpu.VMEM((NOB * UNIT, LANES), jnp.float32),
             pltpu.VMEM((SITES, NOB * UNIT, LANES), jnp.bfloat16),
-            pltpu.SemaphoreType.DMA((2,)),
+            pltpu.SemaphoreType.DMA((4,)),
             pltpu.SemaphoreType.DMA((SITES,)),
             pltpu.SemaphoreType.DMA((SITES,)),
         ],
@@ -81,26 +107,52 @@
             flops=2 * NT * BS * NOB * 4096, bytes_accessed=4 * MIB, transcendentals=0
         ),
         name="pieces",
-    )(pair_mu, three_center, coeff.T)
+    )(pair_mu, pair_site[:, :, 0], pair_pos, three_center, coeff.T)
 
 
 NACC = 4
 
 
-def sum_kernel(key_ref, in_ref, out_ref, *accs):
+FOUR = 4 * UNIT // SUB
+
+
+def sum_kernel(in_ref, out_ref, key_vmem, key_ref, sem, *accs):
+    sub = lax.broadcasted_iota(jnp.int32, (SUB, LANES), 0)
+
+    def tiles_of(two_blocks, wanted):
+        found = {}
+        for pair in sorted({tile // 2 for tile in wanted}):
+            start = pl.multiple_of((two_blocks * FOUR + pair) * 2 * SUB, 2 * SUB)
+            two = in_ref[pl.ds(start, 2 * SUB), :].astype(jnp.float32)
+            found[pair * 2], found[pair * 2 + 1] = two[:SUB], two[SUB:]
+        return found
+
+    keys = jnp.zeros((SUB, LANES), jnp.float32)
+    for u in range(NSRC // 8):
+        found = tiles_of(u, [b * FOUR + 5 * m + 5 for b in range(2) for m in range(4)])
+        for b in range(2):
+            for m in range(4):
+                keys = keys + jnp.where(sub == 2 * m + b, found[b * FOUR + 5 * m + 5], 0.0)
+    key_vmem[...] = keys.astype(jnp.int32)
+    copy = pltpu.make_async_copy(key_vmem, key_ref, sem)
+    copy.start()
     for acc in accs:
         acc[...] = jnp.zeros_like(acc)
-
-    @pl.loop(0, NSRC // 4)
-    def _(i):
-        for pair in range(2 * NT):
-            start = pl.multiple_of(i * 4 * UNIT + pair * 2 * SUB, 2 * SUB)
-            two = in_ref[pl.ds(start, 2 * SUB), :].astype(jnp.float32)
-            for half in range(2):
-                which, t = divmod(pair * 2 + half, NT)
-                acc = accs[(pair * 2 + half) % NACC]
-                where = pl.ds(pl.multiple_of(key_ref[i * 4 + which, t] * SUB, SUB), SUB)
-                acc[where, :] = acc[where, :] + two[half * SUB : (half + 1) * SUB]
+    copy.wait()
+
+    @pl.loop(0, NSRC // 8)
+    def _(u):
+        found = tiles_of(u, range(2 * FOUR))
+        for b in range(2):
+            for m in range(4):
+                for t in range(NT):
+                    tile = found[b * FOUR + 5 * m + t]
+                    if t == 0 and m > 0:
+                        tile = jnp.where(sub >= 2 * m, tile, found[b * FOUR + 5 * m + 5])
+                    acc = accs[(m + t) % NACC]
+                    row = key_ref[2 * m + b, u * 8 + t] * SUB
+                    where = pl.ds(pl.multiple_of(row, SUB), SUB)
+                    acc[where, :] = acc[where, :] + tile
 
     total = accs[0][...]
     for acc in accs[1:]:
@@ -110,22 +162,26 @@
         out_ref[x] = total
 
 
-def make_sums(keys, arrived):
+def make_sums(arrived):
     return pl.pallas_call(
         sum_kernel,
         in_specs=[
-            pl.BlockSpec(memory_space=pltpu.SMEM),
             pl.BlockSpec(memory_space=pltpu.VMEM),
         ],
         out_specs=pl.BlockSpec(memory_space=pltpu.VMEM),
         out_shape=jax.ShapeDtypeStruct((4, BUCKETS * SUB, LANES), jnp.bfloat16),
-        scratch_shapes=[pltpu.VMEM((BUCKETS * SUB, LANES), jnp.float32)] * NACC,
+        scratch_shapes=[
+            pltpu.VMEM((SUB, LANES), jnp.int32),
+            pltpu.SMEM((SUB, LANES), jnp.int32),
+            pltpu.SemaphoreType.DMA,
+        ]
+        + [pltpu.VMEM((BUCKETS * SUB, LANES), jnp.float32)] * NACC,
         compiler_params=pltpu.CompilerParams(vmem_limit_bytes=32 * MIB),
         cost_estimate=pl.CostEstimate(
             flops=NSRC * NT * BLK, bytes_accessed=2 * MIB, transcendentals=0
         ),
         name="sums",
-    )(keys, arrived)
+    )(arrived)
 
 
 HALF = LANES // 2
@@ -174,12 +230,11 @@
 
 
 def local(three_center, pair_mu, pair_site, pair_pos, coeff, fitting):
-    pieces = make_pieces(three_center, pair_mu, coeff)
-    keys = jnp.pad(pair_site[:, :, 0] * NU_SITE + pair_pos, ((0, 0), (0, LANES - NT)))
-    for axis in reversed(ALL_MU):
-        keys = lax.all_gather(keys, axis, axis=0, tiled=True)
-    arrived = lax.all_to_all(pieces, ALL_MU, split_axis=0, concat_axis=0, tiled=True)
-    sums = make_sums(keys, arrived)
+    pieces = make_pieces(three_center, pair_mu, pair_site, pair_pos, coeff)
+    arrived = lax.all_to_all(
+        pieces.reshape(NSRC, UNIT // 2, 2, LANES), ALL_MU, split_axis=0, concat_axis=0, tiled=True
+    )
+    sums = make_sums(arrived.reshape(NSRC * UNIT, LANES))
     gathered = lax.all_to_all(
         sums.reshape(16, NU_SITE * SUB, LANES), FIT, split_axis=0, concat_axis=0, tiled=True
     )
@@ -189,8 +244,8 @@
 
 
 def solution(mesh):
-    fine = Mesh(mesh.devices.reshape(4, 2, 4, 2, 2, 4), ("zh", "zl", "yh", "yl", "c", "x"))
-    mu = ("zh", "zl", "yh", "yl", "c")
+    fine = Mesh(mesh.devices.reshape(8, 4, 2, 2, 4), ("z", "yh", "yl", "c", "x"))
+    mu = ("z", "yh", "yl", "c")
     in_specs = (
         P(mu, None, "x"),
         P(mu, None),

time: 102 us -> 77.9 us (0.76)
  starting transfers between devices: 24.4 us -> 6.11 us
  blocking collectives: 60.7 us -> 55.8 us
    all_gather x5 -> x0, blocking collectives: 60.7 us -> none  [local(): keys = lax.all_gather(keys, axis, axis=0, tiled=True)]
    all_to_all x0 -> x1, blocking collectives: none -> 55.8 us  [local(): lax.all_to_all(pieces.reshape(NSRC, UNIT // 2, 2, LANES), ALL_MU, split_a...]
    all_to_all x1 -> x0, starting transfers between devices: 18.5 us -> none  [local(): lax.all_to_all(pieces, ALL_MU, split_axis=0, concat_axis=0, tiled=True)]
  transfers between devices with their start and end apart: 2 -> 1, of which waited for: 1 -> 1; matrix products, arithmetic and copies ran while one was open for 0% -> 0% of each run, Pallas kernels for 0% -> 0%
where the time goes in v5:
time: 77.9 us; the launch traced here: 77.6 us
  blocking collectives  55.8 us (72%)
  waiting for transfers between devices  8.39 us (11%)
  Pallas kernels  7.28 us (9%)
  starting transfers between devices  6.11 us (8%)
    all_to_all x1, blocking collectives, local(): lax.all_to_all(pieces.reshape(NSRC, UNIT // 2, 2, LANES), ALL_MU, split_a...  55.8 us
    all_to_all x1, waiting for transfers between devices, local(): lax.all_to_all(sums.reshape(16, NU_SITE * SUB, LANES), FIT, split_axis=0,...  8.39 us
    all_to_all x1, starting transfers between devices, local(): lax.all_to_all(sums.reshape(16, NU_SITE * SUB, LANES), FIT, split_axis=0,...  6.11 us
    pallas_call x1, Pallas kernels, make_pieces(): pl.pallas_call(piece_kernel, in_specs=[pl.BlockSpec(memory_space=pl.ANY)]...  3.25 us
    pallas_call x1, Pallas kernels, make_sums(): pl.pallas_call(sum_kernel, in_specs=[pl.BlockSpec(memory_space=pltpu.VMEM...  2.98 us
  transfers between devices with their start and end apart: 1, of which 1 were waited for; matrix products, arithmetic and copies ran while one was open for 0% of the time, Pallas kernels for 0%

profile of v5, /device:TPU:1, one launch (start us, length us, event | category | flops | bytes accessed | tf_op | source)
XLA Modules:
  0.0 77.6 jit_solution(7587138029512112529)
XLA Ops:
  0.0 3.2 %pieces.1 = bf16[5376,128]{1,0:T(8,128)(2,1)} custom-call(s32[1,5]{1,0:T(1,128)} %mu_hbm.1, s32[1,5]{1,0:T(1,128)} %bitcast.12, s32[1,5]{1,0:T(1,128)} %pos_hbm.1, bf16[5,64,4096]{2,1,0:T(8,128)(2,1)} %slab_hbm.1, bf16[32,3072]{1,0:T(8,128)(2,1)} %bitcast.11), custom_call_target="tpu_custom_call" | custom-call | flops 83886080 | bytes 4194304 | tf_op jit(solution)/shard_map/pieces/pallas_call | solution.py:88
  3.3 55.8 %all_to_all.10 = bf16[128,21,2,128]{3,2,1,0:T(2,128)(2,1)S(1)} all-to-all(bf16[128,21,2,128]{3,2,1,0:T(2,128)(2,1)} %bitcast.10), channel_id=1, replica_groups=mesh['z'=8,'yh'=4,'yl'=2,'c'=2,'x'=4] {'yl','c','z','yh'}, dimensions={0} | all-to-all | bytes 2752512 | tf_op jit(solution)/shard_map/all_to_all | solution.py:234
  59.1 0.0 copy-start
  59.1 3.0 %sums.1 = bf16[4,384,128]{2,1,0:T(8,128)(2,1)} custom-call(bf16[5376,128]{1,0:T(8,128)(2,1)S(1)} %bitcast.8), custom_call_target="tpu_custom_call" | custom-call | flops 655360 | bytes 2097152 | tf_op jit(solution)/shard_map/sums/pallas_call | solution.py:166
  62.0 6.1 %all-to-all-start.1 = ((bf16[16,96,128]{2,1,0:T(8,128)(2,1)}), bf16[16,96,128]{2,1,0:T(8,128)(2,1)S(1)}, u32[]{:S(2)}, u32[]{:S(2)}) async-start(bf16[16,96,128]{2,1,0:T(8,128)(2,1)} %bitcast.5), calls=%async_computation.1 | async-start | bytes 786432 | tf_op jit(solution)/shard_map/all_to_all | solution.py:238
  68.2 8.4 %all-to-all-done.1 = bf16[16,96,128]{2,1,0:T(8,128)(2,1)S(1)} async-done(((bf16[16,96,128]{2,1,0:T(8,128)(2,1)}), bf16[16,96,128]{2,1,0:T(8,128)(2,1)S(1)}, u32[]{:S(2)}, u32[]{:S(2)}) %all-to-all-start.1) | async-done | bytes 393248 | tf_op jit(solution)/shard_map/all_to_all | solution.py:238
  76.5 0.0 copy-done
  76.6 1.1 %fit.1 = bf16[12,4096]{1,0:T(8,128)(2,1)} custom-call(s32[1]{0:T(128)} %bitcast.site_ref, bf16[4,4,96,128]{3,2,1,0:T(8,128)(2,1)S(1)} %bitcast.9, bf16[48,64,256]{2,1,0:T(8,128)(2,1)S(1)} %copy-done), custom_call_target="tpu_custom_call" | custom-call | tf_op jit(solution)/shard_map/fit/pallas_call | solution.py:214
Async XLA Ops:
  59.1 17.5 %copy-start = (bf16[48,64,256]{2,1,0:T(8,128)(2,1)S(1)}, bf16[48,64,256]{2,1,0:T(8,128)(2,1)}, u32[]{:S(2)}) copy-start(bf16[48,64,256]{2,1,0:T(8,128)(2,1)} %weight_ref.1) | copy-start | bytes 4718596
  62.0 14.5 %all-to-all-start.1 = ((bf16[16,96,128]{2,1,0:T(8,128)(2,1)}), bf16[16,96,128]{2,1,0:T(8,128)(2,1)S(1)}, u32[]{:S(2)}, u32[]{:S(2)}) async-start(bf16[16,96,128]{2,1,0:T(8,128)(2,1)} %bitcast.5), calls=%async_computation.1 | async-start | bytes 786432 | tf_op jit(solution)/shard_map/all_to_all | solution.py:238

commit v6 on v5

--- a/solution.py
+++ b/solution.py
@@ -11,20 +11,21 @@
 BS = 64
 NOB = 32
 LANES = 128
-NSRC = 128
+NSRC = 64
 BUCKETS = SITES * NU_SITE
 BLK = 1024
 SUB = BLK // LANES
-DATA = NT * SUB
+PAIR = 2 * SUB
+DATA = NT * PAIR
 UNIT = DATA + 2
-ALL_MU = ("yl", "c", "z", "yh")
-FIT = ("x", "yl", "c")
+MAIN = ("yl", "z", "yh")
+FIT = ("x", "yl")
+PART = NOB // 2 * UNIT
 MIB = 2**20
 
 
 def source_index():
-    quarter = lax.axis_index("yl") * 2 + lax.axis_index("c")
-    return (quarter * 8 + lax.axis_index("z")) * 4 + lax.axis_index("yh")
+    return (lax.axis_index("yl") * 8 + lax.axis_index("z")) * 4 + lax.axis_index("yh")
 
 
 def piece_kernel(
@@ -36,9 +37,9 @@
             slab_hbm.at[:, :, pl.ds(q * BLK, BLK)], slab.at[q], ins.at[q]
         )
 
-    def out_copy(q):
-        rows = pl.ds(q * NOB * UNIT, NOB * UNIT)
-        return pltpu.make_async_copy(done.at[q], out_hbm.at[rows, :], outs.at[q])
+    def out_copy(part):
+        rows = pl.ds(part * PART, PART)
+        return pltpu.make_async_copy(done.at[rows, :], out_hbm.at[rows, :], outs.at[part])
 
     smalls = [
         pltpu.make_async_copy(src, dst, small.at[i])
@@ -69,19 +70,25 @@
             jnp.where(block % 2 == 1, both[:, BS:], both[:, :BS]).astype(jnp.bfloat16)
         )
     for q in range(SITES):
+        column, half = divmod(q, 2)
         slab_copy(q).wait()
         for t in range(NT):
             res = jnp.dot(mine[t], slab[q, t], preferred_element_type=jnp.float32)
             for j in range(SUB):
-                place = t * SUB + j - shift
+                place = t * PAIR + half * SUB + j - shift
                 place = jnp.where(place < 0, place + DATA, place)
                 scr[pl.ds(place, NOB, stride=UNIT), :] = res[
                     :, j * LANES : (j + 1) * LANES
                 ]
-        done[q] = scr[...].astype(jnp.bfloat16)
-        out_copy(q).start()
-    for q in range(SITES):
-        out_copy(q).wait()
+        if half == 1:
+            for o in range(2):
+                start = (column * 2 + o) * PART
+                done[start : start + PART, :] = scr[o * PART : (o + 1) * PART, :].astype(
+                    jnp.bfloat16
+                )
+                out_copy(column * 2 + o).start()
+    for part in range(4):
+        out_copy(part).wait()
 
 
 def make_pieces(three_center, pair_mu, pair_site, pair_pos, coeff):
@@ -89,7 +96,7 @@
         piece_kernel,
         in_specs=[pl.BlockSpec(memory_space=pl.ANY)] * 5,
         out_specs=pl.BlockSpec(memory_space=pl.ANY),
-        out_shape=jax.ShapeDtypeStruct((SITES * NOB * UNIT, LANES), jnp.bfloat16),
+        out_shape=jax.ShapeDtypeStruct((4 * PART, LANES), jnp.bfloat16),
         scratch_shapes=[
             pltpu.SMEM((1, NT), jnp.int32),
             pltpu.SMEM((1, NT), jnp.int32),
@@ -97,7 +104,7 @@
             pltpu.VMEM((SITES, NT, BS, BLK), jnp.bfloat16),
             pltpu.VMEM((NOB, 3072), jnp.bfloat16),
             pltpu.VMEM((NOB * UNIT, LANES), jnp.float32),
-            pltpu.VMEM((SITES, NOB * UNIT, LANES), jnp.bfloat16),
+            pltpu.VMEM((4 * PART, LANES), jnp.bfloat16),
             pltpu.SemaphoreType.DMA((4,)),
             pltpu.SemaphoreType.DMA((SITES,)),
             pltpu.SemaphoreType.DMA((SITES,)),
@@ -110,13 +117,13 @@
     )(pair_mu, pair_site[:, :, 0], pair_pos, three_center, coeff.T)
 
 
-NACC = 4
-
-
+COPIES = 2
+STEP = 2 * NT
 FOUR = 4 * UNIT // SUB
-
-
-def sum_kernel(in_ref, out_ref, key_vmem, key_ref, sem, *accs):
+SITE_ROWS = NU_SITE * SUB
+
+
+def sum_kernel(in_ref, keep_ref, send_ref, key_vmem, key_ref, sem, *accs):
     sub = lax.broadcasted_iota(jnp.int32, (SUB, LANES), 0)
 
     def tiles_of(two_blocks, wanted):
@@ -129,10 +136,10 @@
 
     keys = jnp.zeros((SUB, LANES), jnp.float32)
     for u in range(NSRC // 8):
-        found = tiles_of(u, [b * FOUR + 5 * m + 5 for b in range(2) for m in range(4)])
+        found = tiles_of(u, [b * FOUR + STEP * (m + 1) for b in range(2) for m in range(4)])
         for b in range(2):
             for m in range(4):
-                keys = keys + jnp.where(sub == 2 * m + b, found[b * FOUR + 5 * m + 5], 0.0)
+                keys = keys + jnp.where(sub == 2 * m + b, found[b * FOUR + STEP * (m + 1)], 0.0)
     key_vmem[...] = keys.astype(jnp.int32)
     copy = pltpu.make_async_copy(key_vmem, key_ref, sem)
     copy.start()
@@ -146,42 +153,63 @@
         for b in range(2):
             for m in range(4):
                 for t in range(NT):
-                    tile = found[b * FOUR + 5 * m + t]
-                    if t == 0 and m > 0:
-                        tile = jnp.where(sub >= 2 * m, tile, found[b * FOUR + 5 * m + 5])
-                    acc = accs[(m + t) % NACC]
                     row = key_ref[2 * m + b, u * 8 + t] * SUB
                     where = pl.ds(pl.multiple_of(row, SUB), SUB)
-                    acc[where, :] = acc[where, :] + tile
-
-    total = accs[0][...]
-    for acc in accs[1:]:
-        total = total + acc[...]
-    total = total.astype(jnp.bfloat16)
-    for x in range(4):
-        out_ref[x] = total
+                    for half in range(2):
+                        first = b * FOUR + STEP * m
+                        tile = found[first + 2 * t + half]
+                        if t == 0 and half == 0 and m > 0:
+                            tile = jnp.where(sub >= 2 * m, tile, found[first + STEP])
+                        acc = accs[half * COPIES + (m + t) % COPIES]
+                        acc[where, :] = acc[where, :] + tile
+
+    core = lax.axis_index("c")
+    for ref, parity in ((keep_ref, core), (send_ref, 1 - core)):
+        for high in range(2):
+            rows = pl.ds(pl.multiple_of((high * 2 + parity) * SITE_ROWS, SUB), SITE_ROWS)
+            for half in range(2):
+                total = accs[half * COPIES][rows, :]
+                for other in range(1, COPIES):
+                    total = total + accs[half * COPIES + other][rows, :]
+                ref[high, half] = total
 
 
 def make_sums(arrived):
+    part = jax.ShapeDtypeStruct((2, 2, SITE_ROWS, LANES), jnp.float32)
     return pl.pallas_call(
         sum_kernel,
-        in_specs=[
-            pl.BlockSpec(memory_space=pltpu.VMEM),
-        ],
-        out_specs=pl.BlockSpec(memory_space=pltpu.VMEM),
-        out_shape=jax.ShapeDtypeStruct((4, BUCKETS * SUB, LANES), jnp.bfloat16),
+        in_specs=[pl.BlockSpec(memory_space=pltpu.VMEM)],
+        out_specs=[pl.BlockSpec(memory_space=pltpu.VMEM)] * 2,
+        out_shape=[part, part],
         scratch_shapes=[
             pltpu.VMEM((SUB, LANES), jnp.int32),
             pltpu.SMEM((SUB, LANES), jnp.int32),
             pltpu.SemaphoreType.DMA,
         ]
-        + [pltpu.VMEM((BUCKETS * SUB, LANES), jnp.float32)] * NACC,
+        + [pltpu.VMEM((BUCKETS * SUB, LANES), jnp.float32)] * (2 * COPIES),
         compiler_params=pltpu.CompilerParams(vmem_limit_bytes=32 * MIB),
         cost_estimate=pl.CostEstimate(
-            flops=NSRC * NT * BLK, bytes_accessed=2 * MIB, transcendentals=0
+            flops=NSRC * NT * 2 * BLK, bytes_accessed=2 * MIB, transcendentals=0
         ),
         name="sums",
     )(arrived)
+
+
+def join_kernel(keep_ref, got_ref, out_ref):
+    total = (keep_ref[...] + got_ref[...]).astype(jnp.bfloat16)
+    for x in range(4):
+        out_ref[x] = total
+
+
+def make_join(keep, got):
+    return pl.pallas_call(
+        join_kernel,
+        in_specs=[pl.BlockSpec(memory_space=pltpu.VMEM)] * 2,
+        out_specs=pl.BlockSpec(memory_space=pltpu.VMEM),
+        out_shape=jax.ShapeDtypeStruct((4, 2, 2, SITE_ROWS, LANES), jnp.bfloat16),
+        compiler_params=pltpu.CompilerParams(vmem_limit_bytes=32 * MIB),
+        name="join",
+    )(keep, got)
 
 
 HALF = LANES // 2
@@ -232,11 +260,13 @@
 def local(three_center, pair_mu, pair_site, pair_pos, coeff, fitting):
     pieces = make_pieces(three_center, pair_mu, pair_site, pair_pos, coeff)
     arrived = lax.all_to_all(
-        pieces.reshape(NSRC, UNIT // 2, 2, LANES), ALL_MU, split_axis=0, concat_axis=0, tiled=True
+        pieces.reshape(NSRC, UNIT // 2, 2, LANES), MAIN, split_axis=0, concat_axis=0, tiled=True
     )
-    sums = make_sums(arrived.reshape(NSRC * UNIT, LANES))
+    keep, send = make_sums(arrived.reshape(NSRC * UNIT, LANES))
+    got = lax.ppermute(send, "c", [(0, 1), (1, 0)])
+    sums = make_join(keep, got)
     gathered = lax.all_to_all(
-        sums.reshape(16, NU_SITE * SUB, LANES), FIT, split_axis=0, concat_axis=0, tiled=True
+        sums.reshape(8, 2 * SITE_ROWS, LANES), FIT, split_axis=0, concat_axis=0, tiled=True
     )
     site = lax.axis_index("yl") * 2 + lax.axis_index("c")
     result = make_fit(site.reshape(1), gathered.reshape(4, 4, NU_SITE * SUB, LANES), fitting)

time: 77.9 us -> 76.9 us (0.987)
  blocking collectives: 55.8 us -> 49.4 us
  starting transfers between devices: 6.11 us -> 10.9 us
    ppermute x0 -> x1, starting transfers between devices: none -> 6.48 us  [local(): got = lax.ppermute(send, 'c', [(0, 1), (1, 0)])]
    all_to_all x1, blocking collectives: 55.8 us -> 49.4 us  [local(): lax.all_to_all(pieces.reshape(NSRC, UNIT // 2, 2, LANES), MAIN, split_axi...]
    all_to_all x1, starting transfers between devices: 6.11 us -> 4.42 us  [local(): lax.all_to_all(sums.reshape(8, 2 * SITE_ROWS, LANES), FIT, split_axis=0,...]
    pallas_call x1, Pallas kernels: 2.98 us -> 1.74 us  [make_sums(): pl.pallas_call(sum_kernel, in_specs=[pl.BlockSpec(memory_space=pltpu.VMEM...]
    ppermute x0 -> x1, waiting for transfers between devices: none -> 1.05 us  [local(): got = lax.ppermute(send, 'c', [(0, 1), (1, 0)])]
  transfers between devices with their start and end apart: 1 -> 2, of which waited for: 1 -> 2; matrix products, arithmetic and copies ran while one was open for 0% -> 0% of each run, Pallas kernels for 0% -> 0%
where the time goes in v6:
time: 76.9 us; the launch traced here: 76.4 us
  blocking collectives  49.4 us (64%)
  starting transfers between devices  10.9 us (14%)
  waiting for transfers between devices  9.16 us (12%)
  Pallas kernels  6.88 us (9%)
    all_to_all x1, blocking collectives, local(): lax.all_to_all(pieces.reshape(NSRC, UNIT // 2, 2, LANES), MAIN, split_axi...  49.4 us
    all_to_all x1, waiting for transfers between devices, local(): lax.all_to_all(sums.reshape(8, 2 * SITE_ROWS, LANES), FIT, split_axis=0,...  8.11 us
    ppermute x1, starting transfers between devices, local(): got = lax.ppermute(send, 'c', [(0, 1), (1, 0)])  6.48 us
    all_to_all x1, starting transfers between devices, local(): lax.all_to_all(sums.reshape(8, 2 * SITE_ROWS, LANES), FIT, split_axis=0,...  4.42 us
    pallas_call x1, Pallas kernels, make_pieces(): pl.pallas_call(piece_kernel, in_specs=[pl.BlockSpec(memory_space=pl.ANY)]...  3.31 us
    pallas_call x1, Pallas kernels, make_sums(): pl.pallas_call(sum_kernel, in_specs=[pl.BlockSpec(memory_space=pltpu.VMEM...  1.74 us
  transfers between devices with their start and end apart: 2, of which 2 were waited for; matrix products, arithmetic and copies ran while one was open for 0% of the time, Pallas kernels for 0%

profile of v6, /device:TPU:1, one launch (start us, length us, event | category | flops | bytes accessed | tf_op | source)
XLA Modules:
  0.0 76.4 jit_solution(8605209239567531171)
XLA Ops:
  0.0 3.3 %pieces.1 = bf16[5248,128]{1,0:T(8,128)(2,1)} custom-call(s32[1,5]{1,0:T(1,128)} %mu_hbm.1, s32[1,5]{1,0:T(1,128)} %bitcast.12, s32[1,5]{1,0:T(1,128)} %pos_hbm.1, bf16[5,64,4096]{2,1,0:T(8,128)(2,1)} %slab_hbm.1, bf16[32,3072]{1,0:T(8,128)(2,1)} %bitcast.11), custom_call_target="tpu_custom_call" | custom-call | flops 83886080 | bytes 4194304 | tf_op jit(solution)/shard_map/pieces/pallas_call | solution.py:95
  3.3 49.4 %all_to_all.10 = bf16[64,41,2,128]{3,2,1,0:T(2,128)(2,1)S(1)} all-to-all(bf16[64,41,2,128]{3,2,1,0:T(2,128)(2,1)} %bitcast.10), channel_id=1, replica_groups=mesh['z'=8,'yh'=4,'yl'=2,'c'=2,'x'=4] {'yl','z','yh'}, dimensions={0} | all-to-all | bytes 2686976 | tf_op jit(solution)/shard_map/all_to_all | solution.py:262
  52.8 0.0 copy-start
  52.8 1.7 %sums.1 = (f32[2,2,96,128]{3,2,1,0:T(8,128)S(1)}, f32[2,2,96,128]{3,2,1,0:T(8,128)S(1)}) custom-call(bf16[5248,128]{1,0:T(8,128)(2,1)S(1)} %bitcast.8), custom_call_target="tpu_custom_call" | custom-call | flops 655360 | bytes 2097152 | tf_op jit(solution)/shard_map/sums/pallas_call | solution.py:179
  54.5 6.5 %collective-permute-start = (f32[2,2,96,128]{3,2,1,0:T(8,128)S(1)}, f32[2,2,96,128]{3,2,1,0:T(8,128)S(1)}, u32[]{:S(2)}, u32[]{:S(2)}) collective-permute-start(f32[2,2,96,128]{3,2,1,0:T(8,128)S(1)} %get-tuple-element.8), channel_id=1, source_target_pairs={{0,4},{4,0},{1,5},{5,1},{2,6},{6,2},{3,7},{7,3},{8,12},{12,8},{9,1... | collective-permute-start | bytes 589832 | tf_op jit(solution)/shard_map/ppermute | solution.py:266
  61.0 1.0 %collective-permute-done.got_ref = f32[2,2,96,128]{3,2,1,0:T(8,128)S(1)} collective-permute-done((f32[2,2,96,128]{3,2,1,0:T(8,128)S(1)}, f32[2,2,96,128]{3,2,1,0:T(8,128)S(1)}, u32[]{:S(2)}, u32[]{:S(2)}) %collective-permute-start) | collective-permute-done | bytes 196640 | tf_op jit(solution)/shard_map/ppermute | solution.py:266
  62.0 0.8 %join.1 = bf16[4,2,2,96,128]{4,3,2,1,0:T(8,128)(2,1)} custom-call(f32[2,2,96,128]{3,2,1,0:T(8,128)S(1)} %get-tuple-element.7.keep_ref, f32[2,2,96,128]{3,2,1,0:T(8,128)S(1)} %collective-permute-done.got_ref), custom_call_target="tpu_custom_call" | custom-call | tf_op jit(solution)/shard_map/join/pallas_call | solution.py:205
  62.8 4.4 %all-to-all-start.1 = ((bf16[8,192,128]{2,1,0:T(8,128)(2,1)}), bf16[8,192,128]{2,1,0:T(8,128)(2,1)S(1)}, u32[]{:S(2)}, u32[]{:S(2)}) async-start(bf16[8,192,128]{2,1,0:T(8,128)(2,1)} %bitcast.5), calls=%async_computation.1 | async-start | bytes 786432 | tf_op jit(solution)/shard_map/all_to_all | solution.py:268
  67.2 8.1 %all-to-all-done.1 = bf16[8,192,128]{2,1,0:T(8,128)(2,1)S(1)} async-done(((bf16[8,192,128]{2,1,0:T(8,128)(2,1)}), bf16[8,192,128]{2,1,0:T(8,128)(2,1)S(1)}, u32[]{:S(2)}, u32[]{:S(2)}) %all-to-all-start.1) | async-done | bytes 393248 | tf_op jit(solution)/shard_map/all_to_all | solution.py:268
  75.3 0.0 copy-done
  75.3 1.1 %fit.1 = bf16[12,4096]{1,0:T(8,128)(2,1)} custom-call(s32[1]{0:T(128)} %bitcast.site_ref, bf16[4,4,96,128]{3,2,1,0:T(8,128)(2,1)S(1)} %bitcast.9, bf16[48,64,256]{2,1,0:T(8,128)(2,1)S(1)} %copy-done), custom_call_target="tpu_custom_call" | custom-call | tf_op jit(solution)/shard_map/fit/pallas_call | solution.py:242
Async XLA Ops:
  52.8 22.6 %copy-start = (bf16[48,64,256]{2,1,0:T(8,128)(2,1)S(1)}, bf16[48,64,256]{2,1,0:T(8,128)(2,1)}, u32[]{:S(2)}) copy-start(bf16[48,64,256]{2,1,0:T(8,128)(2,1)} %weight_ref.1) | copy-start | bytes 4718596
  54.5 7.5 %collective-permute-start = (f32[2,2,96,128]{3,2,1,0:T(8,128)S(1)}, f32[2,2,96,128]{3,2,1,0:T(8,128)S(1)}, u32[]{:S(2)}, u32[]{:S(2)}) collective-permute-start(f32[2,2,96,128]{3,2,1,0:T(8,128)S(1)} %get-tuple-element.8), channel_id=1, source_target_pairs={{0,4},{4,0},{1,5},{5,1},{2,6},{6,2},{3,7},{7,3},{8,12},{12,8},{9,1... | collective-permute-start | bytes 589832 | tf_op jit(solution)/shard_map/ppermute | solution.py:266
  62.8 12.5 %all-to-all-start.1 = ((bf16[8,192,128]{2,1,0:T(8,128)(2,1)}), bf16[8,192,128]{2,1,0:T(8,128)(2,1)S(1)}, u32[]{:S(2)}, u32[]{:S(2)}) async-start(bf16[8,192,128]{2,1,0:T(8,128)(2,1)} %bitcast.5), calls=%async_computation.1 | async-start | bytes 786432 | tf_op jit(solution)/shard_map/all_to_all | solution.py:268

commit v7 on v6

--- a/solution.py
+++ b/solution.py
@@ -195,13 +195,13 @@
     )(arrived)
 
 
-def join_kernel(keep_ref, got_ref, out_ref):
-    total = (keep_ref[...] + got_ref[...]).astype(jnp.bfloat16)
+def join_kernel(keep_ref, both_ref, out_ref):
+    total = (keep_ref[...] + both_ref[1 - lax.axis_index("c")]).astype(jnp.bfloat16)
     for x in range(4):
         out_ref[x] = total
 
 
-def make_join(keep, got):
+def make_join(keep, both):
     return pl.pallas_call(
         join_kernel,
         in_specs=[pl.BlockSpec(memory_space=pltpu.VMEM)] * 2,
@@ -209,7 +209,7 @@
         out_shape=jax.ShapeDtypeStruct((4, 2, 2, SITE_ROWS, LANES), jnp.bfloat16),
         compiler_params=pltpu.CompilerParams(vmem_limit_bytes=32 * MIB),
         name="join",
-    )(keep, got)
+    )(keep, both)
 
 
 HALF = LANES // 2
@@ -263,8 +263,8 @@
         pieces.reshape(NSRC, UNIT // 2, 2, LANES), MAIN, split_axis=0, concat_axis=0, tiled=True
     )
     keep, send = make_sums(arrived.reshape(NSRC * UNIT, LANES))
-    got = lax.ppermute(send, "c", [(0, 1), (1, 0)])
-    sums = make_join(keep, got)
+    both = lax.all_gather(send, "c", axis=0)
+    sums = make_join(keep, both)
     gathered = lax.all_to_all(
         sums.reshape(8, 2 * SITE_ROWS, LANES), FIT, split_axis=0, concat_axis=0, tiled=True
     )

time: 76.9 us -> 75.7 us (0.984)
  starting transfers between devices: 10.9 us -> 4.42 us
  blocking collectives: 49.4 us -> 55.7 us
  waiting for transfers between devices: 9.16 us -> 8.11 us
    ppermute x1 -> x0, starting transfers between devices: 6.48 us -> none  [local(): got = lax.ppermute(send, 'c', [(0, 1), (1, 0)])]
    all_gather x0 -> x1, blocking collectives: none -> 6.29 us  [local(): both = lax.all_gather(send, 'c', axis=0)]
    ppermute x1 -> x0, waiting for transfers between devices: 1.05 us -> none  [local(): got = lax.ppermute(send, 'c', [(0, 1), (1, 0)])]
  transfers between devices with their start and end apart: 2 -> 1, of which waited for: 2 -> 1; matrix products, arithmetic and copies ran while one was open for 0% -> 0% of each run, Pallas kernels for 0% -> 0%
where the time goes in v7:
time: 75.7 us; the launch traced here: 75.2 us
  blocking collectives  55.7 us (74%)
  waiting for transfers between devices  8.11 us (11%)
  Pallas kernels  6.88 us (9%)
  starting transfers between devices  4.42 us (6%)
    all_to_all x1, blocking collectives, local(): lax.all_to_all(pieces.reshape(NSRC, UNIT // 2, 2, LANES), MAIN, split_axi...  49.4 us
    all_to_all x1, waiting for transfers between devices, local(): lax.all_to_all(sums.reshape(8, 2 * SITE_ROWS, LANES), FIT, split_axis=0,...  8.11 us
    all_gather x1, blocking collectives, local(): both = lax.all_gather(send, 'c', axis=0)  6.29 us
    all_to_all x1, starting transfers between devices, local(): lax.all_to_all(sums.reshape(8, 2 * SITE_ROWS, LANES), FIT, split_axis=0,...  4.42 us
    pallas_call x1, Pallas kernels, make_pieces(): pl.pallas_call(piece_kernel, in_specs=[pl.BlockSpec(memory_space=pl.ANY)]...  3.3 us
    pallas_call x1, Pallas kernels, make_sums(): pl.pallas_call(sum_kernel, in_specs=[pl.BlockSpec(memory_space=pltpu.VMEM...  1.74 us
  transfers between devices with their start and end apart: 1, of which 1 were waited for; matrix products, arithmetic and copies ran while one was open for 0% of the time, Pallas kernels for 0%

profile of v7, /device:TPU:1, one launch (start us, length us, event | category | flops | bytes accessed | tf_op | source)
XLA Modules:
  0.0 75.2 jit_solution(15199184549160039893)
XLA Ops:
  0.0 3.3 %pieces.1 = bf16[5248,128]{1,0:T(8,128)(2,1)} custom-call(s32[1,5]{1,0:T(1,128)} %mu_hbm.1, s32[1,5]{1,0:T(1,128)} %bitcast.14, s32[1,5]{1,0:T(1,128)} %pos_hbm.1, bf16[5,64,4096]{2,1,0:T(8,128)(2,1)} %slab_hbm.1, bf16[32,3072]{1,0:T(8,128)(2,1)} %bitcast.13), custom_call_target="tpu_custom_call" | custom-call | flops 83886080 | bytes 4194304 | tf_op jit(solution)/shard_map/pieces/pallas_call | solution.py:95
  3.3 49.4 %all_to_all.10 = bf16[64,41,2,128]{3,2,1,0:T(2,128)(2,1)S(1)} all-to-all(bf16[64,41,2,128]{3,2,1,0:T(2,128)(2,1)} %bitcast.12), channel_id=1, replica_groups=mesh['z'=8,'yh'=4,'yl'=2,'c'=2,'x'=4] {'yl','z','yh'}, dimensions={0} | all-to-all | bytes 2686976 | tf_op jit(solution)/shard_map/all_to_all | solution.py:262
  52.7 0.0 copy-start
  52.7 1.7 %sums.1 = (f32[2,2,96,128]{3,2,1,0:T(8,128)S(1)}, f32[2,2,96,128]{3,2,1,0:T(8,128)S(1)}) custom-call(bf16[5248,128]{1,0:T(8,128)(2,1)S(1)} %bitcast.9), custom_call_target="tpu_custom_call" | custom-call | flops 655360 | bytes 2097152 | tf_op jit(solution)/shard_map/sums/pallas_call | solution.py:179
  54.5 6.3 %all-gather = f32[4,2,96,128]{3,2,1,0:T(8,128)S(1)} all-gather(f32[2,2,96,128]{3,2,1,0:T(8,128)S(1)} %get-tuple-element.8), channel_id=2, replica_groups=mesh['z'=8,'yh'=4,'yl'=2,'c'=2,'x'=4] {'c'}, dimensions={0}, use_global_device_ids=true | all-gather | bytes 589824 | tf_op jit(solution)/shard_map/all_gather | solution.py:266
  60.8 0.8 %join.1 = bf16[4,2,2,96,128]{4,3,2,1,0:T(8,128)(2,1)} custom-call(f32[2,2,96,128]{3,2,1,0:T(8,128)S(1)} %get-tuple-element.7.keep_ref, f32[2,2,2,96,128]{4,3,2,1,0:T(8,128)S(1)} %bitcast.11), custom_call_target="tpu_custom_call" | custom-call | tf_op jit(solution)/shard_map/join/pallas_call | solution.py:205
  61.6 4.4 %all-to-all-start.1 = ((bf16[8,192,128]{2,1,0:T(8,128)(2,1)}), bf16[8,192,128]{2,1,0:T(8,128)(2,1)S(1)}, u32[]{:S(2)}, u32[]{:S(2)}) async-start(bf16[8,192,128]{2,1,0:T(8,128)(2,1)} %bitcast.6), calls=%async_computation.1 | async-start | bytes 786432 | tf_op jit(solution)/shard_map/all_to_all | solution.py:268
  66.0 8.1 %all-to-all-done.1 = bf16[8,192,128]{2,1,0:T(8,128)(2,1)S(1)} async-done(((bf16[8,192,128]{2,1,0:T(8,128)(2,1)}), bf16[8,192,128]{2,1,0:T(8,128)(2,1)S(1)}, u32[]{:S(2)}, u32[]{:S(2)}) %all-to-all-start.1) | async-done | bytes 393248 | tf_op jit(solution)/shard_map/all_to_all | solution.py:268
  74.1 0.0 copy-done
  74.1 1.1 %fit.1 = bf16[12,4096]{1,0:T(8,128)(2,1)} custom-call(s32[1]{0:T(128)} %bitcast.site_ref, bf16[4,4,96,128]{3,2,1,0:T(8,128)(2,1)S(1)} %bitcast.10, bf16[48,64,256]{2,1,0:T(8,128)(2,1)S(1)} %copy-done), custom_call_target="tpu_custom_call" | custom-call | tf_op jit(solution)/shard_map/fit/pallas_call | solution.py:242
Async XLA Ops:
  52.7 21.4 %copy-start = (bf16[48,64,256]{2,1,0:T(8,128)(2,1)S(1)}, bf16[48,64,256]{2,1,0:T(8,128)(2,1)}, u32[]{:S(2)}) copy-start(bf16[48,64,256]{2,1,0:T(8,128)(2,1)} %weight_ref.1) | copy-start | bytes 4718596
  61.6 12.5 %all-to-all-start.1 = ((bf16[8,192,128]{2,1,0:T(8,128)(2,1)}), bf16[8,192,128]{2,1,0:T(8,128)(2,1)S(1)}, u32[]{:S(2)}, u32[]{:S(2)}) async-start(bf16[8,192,128]{2,1,0:T(8,128)(2,1)} %bitcast.6), calls=%async_computation.1 | async-start | bytes 786432 | tf_op jit(solution)/shard_map/all_to_all | solution.py:268

commit v8 on v7

--- a/solution.py
+++ b/solution.py
@@ -20,7 +20,6 @@
 UNIT = DATA + 2
 MAIN = ("yl", "z", "yh")
 FIT = ("x", "yl")
-PART = NOB // 2 * UNIT
 MIB = 2**20
 
 
@@ -29,17 +28,13 @@
 
 
 def piece_kernel(
-    mu_hbm, site_hbm, pos_hbm, slab_hbm, coeff_hbm, out_hbm,
-    mu, site, pos, slab, coeff, scr, done, small, ins, outs,
+    mu_hbm, site_hbm, pos_hbm, slab_hbm, coeff_hbm, out_ref,
+    mu, site, pos, slab, coeff, scr, small, ins,
 ):
     def slab_copy(q):
         return pltpu.make_async_copy(
             slab_hbm.at[:, :, pl.ds(q * BLK, BLK)], slab.at[q], ins.at[q]
         )
-
-    def out_copy(part):
-        rows = pl.ds(part * PART, PART)
-        return pltpu.make_async_copy(done.at[rows, :], out_hbm.at[rows, :], outs.at[part])
 
     smalls = [
         pltpu.make_async_copy(src, dst, small.at[i])
@@ -81,22 +76,16 @@
                     :, j * LANES : (j + 1) * LANES
                 ]
         if half == 1:
-            for o in range(2):
-                start = (column * 2 + o) * PART
-                done[start : start + PART, :] = scr[o * PART : (o + 1) * PART, :].astype(
-                    jnp.bfloat16
-                )
-                out_copy(column * 2 + o).start()
-    for part in range(4):
-        out_copy(part).wait()
+            start = column * NOB * UNIT
+            out_ref[start : start + NOB * UNIT, :] = scr[...].astype(jnp.bfloat16)
 
 
 def make_pieces(three_center, pair_mu, pair_site, pair_pos, coeff):
     return pl.pallas_call(
         piece_kernel,
-        in_specs=[pl.BlockSpec(memory_space=pl.ANY)] * 5,
-        out_specs=pl.BlockSpec(memory_space=pl.ANY),
-        out_shape=jax.ShapeDtypeStruct((4 * PART, LANES), jnp.bfloat16),
+        in_specs=[pl.BlockSpec(memory_space=pltpu.HBM)] * 5,
+        out_specs=pl.BlockSpec(memory_space=pltpu.VMEM),
+        out_shape=pltpu.VMEM((2 * NOB * UNIT, LANES), jnp.bfloat16),
         scratch_shapes=[
             pltpu.SMEM((1, NT), jnp.int32),
             pltpu.SMEM((1, NT), jnp.int32),
@@ -104,9 +93,7 @@
             pltpu.VMEM((SITES, NT, BS, BLK), jnp.bfloat16),
             pltpu.VMEM((NOB, 3072), jnp.bfloat16),
             pltpu.VMEM((NOB * UNIT, LANES), jnp.float32),
-            pltpu.VMEM((4 * PART, LANES), jnp.bfloat16),
             pltpu.SemaphoreType.DMA((4,)),
-            pltpu.SemaphoreType.DMA((SITES,)),
             pltpu.SemaphoreType.DMA((SITES,)),
         ],
         compiler_params=pltpu.CompilerParams(vmem_limit_bytes=58 * MIB),

time: 75.7 us -> 74.6 us (0.985)
  Pallas kernels: 6.88 us -> 6.04 us
    pallas_call x1, Pallas kernels: 3.3 us -> 2.46 us  [make_pieces(): pl.pallas_call(piece_kernel, in_specs=[pl.BlockSpec(memory_space=pltpu.HB...]
where the time goes in v8:
time: 74.6 us; the launch traced here: 74.1 us
  blocking collectives  55.5 us (74%)
  waiting for transfers between devices  8.11 us (11%)
  Pallas kernels  6.04 us (8%)
  starting transfers between devices  4.42 us (6%)
    all_to_all x1, blocking collectives, local(): lax.all_to_all(pieces.reshape(NSRC, UNIT // 2, 2, LANES), MAIN, split_axi...  49.2 us
    all_to_all x1, waiting for transfers between devices, local(): lax.all_to_all(sums.reshape(8, 2 * SITE_ROWS, LANES), FIT, split_axis=0,...  8.11 us
    all_gather x1, blocking collectives, local(): both = lax.all_gather(send, 'c', axis=0)  6.29 us
    all_to_all x1, starting transfers between devices, local(): lax.all_to_all(sums.reshape(8, 2 * SITE_ROWS, LANES), FIT, split_axis=0,...  4.42 us
    pallas_call x1, Pallas kernels, make_pieces(): pl.pallas_call(piece_kernel, in_specs=[pl.BlockSpec(memory_space=pltpu.HB...  2.46 us
    pallas_call x1, Pallas kernels, make_sums(): pl.pallas_call(sum_kernel, in_specs=[pl.BlockSpec(memory_space=pltpu.VMEM...  1.74 us
  transfers between devices with their start and end apart: 1, of which 1 were waited for; matrix products, arithmetic and copies ran while one was open for 0% of the time, Pallas kernels for 0%

profile of v8, /device:TPU:1, one launch (start us, length us, event | category | flops | bytes accessed | tf_op | source)
XLA Modules:
  0.0 74.1 jit_solution(2248188958085022057)
XLA Ops:
  0.0 2.5 %pieces.1 = bf16[5248,128]{1,0:T(8,128)(2,1)S(1)} custom-call(s32[1,5]{1,0:T(1,128)} %mu_hbm.1, s32[1,5]{1,0:T(1,128)} %bitcast.14, s32[1,5]{1,0:T(1,128)} %pos_hbm.1, bf16[5,64,4096]{2,1,0:T(8,128)(2,1)} %slab_hbm.1, bf16[32,3072]{1,0:T(8,128)(2,1)} %bitcast.13), custom_call_target="tpu_custom_call" | custom-call | flops 83886080 | bytes 4194304 | tf_op jit(solution)/shard_map/pieces/pallas_call | solution.py:84
  2.5 49.2 %all_to_all.10 = bf16[64,41,2,128]{3,2,1,0:T(2,128)(2,1)S(1)} all-to-all(bf16[64,41,2,128]{3,2,1,0:T(2,128)(2,1)S(1)} %bitcast.9), channel_id=1, replica_groups=mesh['z'=8,'yh'=4,'yl'=2,'c'=2,'x'=4] {'yl','z','yh'}, dimensions={0} | all-to-all | bytes 2686976 | tf_op jit(solution)/shard_map/all_to_all | solution.py:249
  51.7 0.0 copy-start
  51.7 1.7 %sums.1 = (f32[2,2,96,128]{3,2,1,0:T(8,128)S(1)}, f32[2,2,96,128]{3,2,1,0:T(8,128)S(1)}) custom-call(bf16[5248,128]{1,0:T(8,128)(2,1)S(1)} %bitcast.10), custom_call_target="tpu_custom_call" | custom-call | flops 655360 | bytes 2097152 | tf_op jit(solution)/shard_map/sums/pallas_call | solution.py:166
  53.4 6.3 %all-gather = f32[4,2,96,128]{3,2,1,0:T(8,128)S(1)} all-gather(f32[2,2,96,128]{3,2,1,0:T(8,128)S(1)} %get-tuple-element.8), channel_id=2, replica_groups=mesh['z'=8,'yh'=4,'yl'=2,'c'=2,'x'=4] {'c'}, dimensions={0}, use_global_device_ids=true | all-gather | bytes 589824 | tf_op jit(solution)/shard_map/all_gather | solution.py:253
  59.7 0.8 %join.1 = bf16[4,2,2,96,128]{4,3,2,1,0:T(8,128)(2,1)} custom-call(f32[2,2,96,128]{3,2,1,0:T(8,128)S(1)} %get-tuple-element.7.keep_ref, f32[2,2,2,96,128]{4,3,2,1,0:T(8,128)S(1)} %bitcast.12), custom_call_target="tpu_custom_call" | custom-call | tf_op jit(solution)/shard_map/join/pallas_call | solution.py:192
  60.5 4.4 %all-to-all-start.1 = ((bf16[8,192,128]{2,1,0:T(8,128)(2,1)}), bf16[8,192,128]{2,1,0:T(8,128)(2,1)S(1)}, u32[]{:S(2)}, u32[]{:S(2)}) async-start(bf16[8,192,128]{2,1,0:T(8,128)(2,1)} %bitcast.6), calls=%async_computation.1 | async-start | bytes 786432 | tf_op jit(solution)/shard_map/all_to_all | solution.py:255
  64.9 8.1 %all-to-all-done.1 = bf16[8,192,128]{2,1,0:T(8,128)(2,1)S(1)} async-done(((bf16[8,192,128]{2,1,0:T(8,128)(2,1)}), bf16[8,192,128]{2,1,0:T(8,128)(2,1)S(1)}, u32[]{:S(2)}, u32[]{:S(2)}) %all-to-all-start.1) | async-done | bytes 393248 | tf_op jit(solution)/shard_map/all_to_all | solution.py:255
  73.0 0.0 copy-done
  73.1 1.1 %fit.1 = bf16[12,4096]{1,0:T(8,128)(2,1)} custom-call(s32[1]{0:T(128)} %bitcast.site_ref, bf16[4,4,96,128]{3,2,1,0:T(8,128)(2,1)S(1)} %bitcast.11, bf16[48,64,256]{2,1,0:T(8,128)(2,1)S(1)} %copy-done), custom_call_target="tpu_custom_call" | custom-call | tf_op jit(solution)/shard_map/fit/pallas_call | solution.py:229
Async XLA Ops:
  51.7 21.4 %copy-start = (bf16[48,64,256]{2,1,0:T(8,128)(2,1)S(1)}, bf16[48,64,256]{2,1,0:T(8,128)(2,1)}, u32[]{:S(2)}) copy-start(bf16[48,64,256]{2,1,0:T(8,128)(2,1)} %weight_ref.1) | copy-start | bytes 4718596
  60.5 12.5 %all-to-all-start.1 = ((bf16[8,192,128]{2,1,0:T(8,128)(2,1)}), bf16[8,192,128]{2,1,0:T(8,128)(2,1)S(1)}, u32[]{:S(2)}, u32[]{:S(2)}) async-start(bf16[8,192,128]{2,1,0:T(8,128)(2,1)} %bitcast.6), calls=%async_computation.1 | async-start | bytes 786432 | tf_op jit(solution)/shard_map/all_to_all | solution.py:255

commit v9 on v8

--- a/solution.py
+++ b/solution.py
@@ -204,7 +204,8 @@
 KPAD = 16
 
 
-def fit_kernel(site_ref, in_ref, weight_ref, out_ref, scr):
+def fit_kernel(in_ref, weight_ref, out_ref, scr):
+    site = lax.axis_index("yl") * 2 + lax.axis_index("c")
     for k in range(NU_SITE):
         rows = [
             jnp.concatenate([in_ref[x, q, pl.ds(k * SUB, SUB), :] for q in range(4)], axis=0)
@@ -214,7 +215,7 @@
         high = jnp.concatenate([r[:, HALF:] for r in rows], axis=1)
         res = lax.dot_general(
             jnp.concatenate([low, high], axis=0),
-            weight_ref[k],
+            weight_ref[site * NU_SITE + k],
             (((1,), (1,)), ((), ())),
             preferred_element_type=jnp.float32,
         )
@@ -225,23 +226,16 @@
         )
 
 
-def make_fit(site, gathered, fitting):
+def make_fit(gathered, fitting):
     return pl.pallas_call(
         fit_kernel,
-        grid_spec=pltpu.PrefetchScalarGridSpec(
-            num_scalar_prefetch=1,
-            grid=(1,),
-            in_specs=[
-                pl.BlockSpec((4, 4, NU_SITE * SUB, LANES), lambda i, site: (0, 0, 0, 0)),
-                pl.BlockSpec((NU_SITE, 64, 256), lambda i, site: (site[0], 0, 0)),
-            ],
-            out_specs=pl.BlockSpec((NU_SITE, NHI * LANES), lambda i, site: (0, 0)),
-            scratch_shapes=[pltpu.VMEM((NHI * KPAD, LANES), jnp.float32)],
-        ),
+        in_specs=[pl.BlockSpec(memory_space=pltpu.VMEM)] * 2,
+        out_specs=pl.BlockSpec(memory_space=pltpu.VMEM),
         out_shape=jax.ShapeDtypeStruct((NU_SITE, NHI * LANES), jnp.bfloat16),
+        scratch_shapes=[pltpu.VMEM((NHI * KPAD, LANES), jnp.float32)],
         compiler_params=pltpu.CompilerParams(vmem_limit_bytes=32 * MIB),
         name="fit",
-    )(site, gathered, fitting)
+    )(gathered, fitting)
 
 
 def local(three_center, pair_mu, pair_site, pair_pos, coeff, fitting):
@@ -255,8 +249,7 @@
     gathered = lax.all_to_all(
         sums.reshape(8, 2 * SITE_ROWS, LANES), FIT, split_axis=0, concat_axis=0, tiled=True
     )
-    site = lax.axis_index("yl") * 2 + lax.axis_index("c")
-    result = make_fit(site.reshape(1), gathered.reshape(4, 4, NU_SITE * SUB, LANES), fitting)
+    result = make_fit(gathered.reshape(4, 4, NU_SITE * SUB, LANES), fitting)
     return result.reshape(1, NU_SITE, 1, 4096)
 
 

time: 74.6 us -> 73.7 us (0.988)
  blocking collectives: 55.5 us -> 67.6 us
  waiting for transfers between devices: 8.11 us -> 0 us
  starting transfers between devices: 4.42 us -> 0 us
  Pallas kernels: 6.04 us -> 5.29 us
    all_to_all x0 -> x1, blocking collectives: none -> 12.1 us  [local(): lax.all_to_all(sums.reshape(8, 2 * SITE_ROWS, LANES), FIT, split_axis=0,...]
    all_to_all x1 -> x0, waiting for transfers between devices: 8.11 us -> none  [local(): lax.all_to_all(sums.reshape(8, 2 * SITE_ROWS, LANES), FIT, split_axis=0,...]
    all_to_all x1 -> x0, starting transfers between devices: 4.42 us -> none  [local(): lax.all_to_all(sums.reshape(8, 2 * SITE_ROWS, LANES), FIT, split_axis=0,...]
    pallas_call x1, Pallas kernels: 0.78 us -> 0.03 us  [make_join(): pl.pallas_call(join_kernel, in_specs=[pl.BlockSpec(memory_space=pltpu.VME...]
  transfers between devices with their start and end apart: 1 -> 0, of which waited for: 1 -> 0; matrix products, arithmetic and copies ran while one was open for 0% -> 0% of each run, Pallas kernels for 0% -> 0%
where the time goes in v9:
time: 73.7 us; the launch traced here: 72.9 us
  blocking collectives  67.6 us (92%)
  Pallas kernels  5.29 us (7%)
    all_to_all x1, blocking collectives, local(): lax.all_to_all(pieces.reshape(NSRC, UNIT // 2, 2, LANES), MAIN, split_axi...  49.2 us
    all_to_all x1, blocking collectives, local(): lax.all_to_all(sums.reshape(8, 2 * SITE_ROWS, LANES), FIT, split_axis=0,...  12.1 us
    all_gather x1, blocking collectives, local(): both = lax.all_gather(send, 'c', axis=0)  6.29 us
    pallas_call x1, Pallas kernels, make_pieces(): pl.pallas_call(piece_kernel, in_specs=[pl.BlockSpec(memory_space=pltpu.HB...  2.46 us
    pallas_call x1, Pallas kernels, make_sums(): pl.pallas_call(sum_kernel, in_specs=[pl.BlockSpec(memory_space=pltpu.VMEM...  1.74 us

profile of v9, /device:TPU:1, one launch (start us, length us, event | category | flops | bytes accessed | tf_op | source)
XLA Modules:
  0.0 72.9 jit_solution(7265085939029434685)
XLA Ops:
  0.0 2.5 %pieces.1 = bf16[5248,128]{1,0:T(8,128)(2,1)S(1)} custom-call(s32[1,5]{1,0:T(1,128)} %mu_hbm.1, s32[1,5]{1,0:T(1,128)} %bitcast.14, s32[1,5]{1,0:T(1,128)} %pos_hbm.1, bf16[5,64,4096]{2,1,0:T(8,128)(2,1)} %slab_hbm.1, bf16[32,3072]{1,0:T(8,128)(2,1)} %bitcast.13), custom_call_target="tpu_custom_call" | custom-call | flops 83886080 | bytes 4194304 | tf_op jit(solution)/shard_map/pieces/pallas_call | solution.py:84
  2.5 49.2 %all_to_all.10 = bf16[64,41,2,128]{3,2,1,0:T(2,128)(2,1)S(1)} all-to-all(bf16[64,41,2,128]{3,2,1,0:T(2,128)(2,1)S(1)} %bitcast.8), channel_id=1, replica_groups=mesh['z'=8,'yh'=4,'yl'=2,'c'=2,'x'=4] {'yl','z','yh'}, dimensions={0} | all-to-all | bytes 2686976 | tf_op jit(solution)/shard_map/all_to_all | solution.py:243
  51.7 0.0 copy-start
  51.7 1.7 %sums.1 = (f32[2,2,96,128]{3,2,1,0:T(8,128)S(1)}, f32[2,2,96,128]{3,2,1,0:T(8,128)S(1)}) custom-call(bf16[5248,128]{1,0:T(8,128)(2,1)S(1)} %bitcast.9), custom_call_target="tpu_custom_call" | custom-call | flops 655360 | bytes 2097152 | tf_op jit(solution)/shard_map/sums/pallas_call | solution.py:166
  53.4 6.3 %all-gather = f32[4,2,96,128]{3,2,1,0:T(8,128)S(1)} all-gather(f32[2,2,96,128]{3,2,1,0:T(8,128)S(1)} %get-tuple-element.8), channel_id=2, replica_groups=mesh['z'=8,'yh'=4,'yl'=2,'c'=2,'x'=4] {'c'}, dimensions={0}, use_global_device_ids=true | all-gather | bytes 589824 | tf_op jit(solution)/shard_map/all_gather | solution.py:247
  59.8 12.1 %all_to_all.11 = bf16[8,192,128]{2,1,0:T(8,128)(2,1)S(1)} all-to-all(bf16[8,192,128]{2,1,0:T(8,128)(2,1)S(1)} %bitcast.12), channel_id=1, replica_groups=mesh['z'=8,'yh'=4,'yl'=2,'c'=2,'x'=4] {'x','yl'}, dimensions={0} | all-to-all | bytes 786432 | tf_op jit(solution)/shard_map/all_to_all | solution.py:249
  71.8 0.0 copy-done
  71.8 1.1 %fit.1 = bf16[12,4096]{1,0:T(8,128)(2,1)} custom-call(bf16[4,4,96,128]{3,2,1,0:T(8,128)(2,1)S(1)} %bitcast.10, bf16[48,64,256]{2,1,0:T(8,128)(2,1)S(1)} %copy-done), custom_call_target="tpu_custom_call" | custom-call | tf_op jit(solution)/shard_map/fit/pallas_call | solution.py:230
  (1 shorter events, 0.0 us)
Async XLA Ops:
  51.7 20.1 %copy-start = (bf16[48,64,256]{2,1,0:T(8,128)(2,1)S(1)}, bf16[48,64,256]{2,1,0:T(8,128)(2,1)}, u32[]{:S(2)}) copy-start(bf16[48,64,256]{2,1,0:T(8,128)(2,1)} %weight_ref.1) | copy-start | bytes 4718596

commit v10 on v9

--- a/solution.py
+++ b/solution.py
@@ -158,16 +158,19 @@
                 total = accs[half * COPIES][rows, :]
                 for other in range(1, COPIES):
                     total = total + accs[half * COPIES + other][rows, :]
-                ref[high, half] = total
+                ref[high, half] = total.astype(ref.dtype)
 
 
 def make_sums(arrived):
-    part = jax.ShapeDtypeStruct((2, 2, SITE_ROWS, LANES), jnp.float32)
+    shape = (2, 2, SITE_ROWS, LANES)
     return pl.pallas_call(
         sum_kernel,
         in_specs=[pl.BlockSpec(memory_space=pltpu.VMEM)],
         out_specs=[pl.BlockSpec(memory_space=pltpu.VMEM)] * 2,
-        out_shape=[part, part],
+        out_shape=[
+            jax.ShapeDtypeStruct(shape, jnp.float32),
+            jax.ShapeDtypeStruct(shape, jnp.bfloat16),
+        ],
         scratch_shapes=[
             pltpu.VMEM((SUB, LANES), jnp.int32),
             pltpu.SMEM((SUB, LANES), jnp.int32),
@@ -183,7 +186,8 @@
 
 
 def join_kernel(keep_ref, both_ref, out_ref):
-    total = (keep_ref[...] + both_ref[1 - lax.axis_index("c")]).astype(jnp.bfloat16)
+    got = both_ref[1 - lax.axis_index("c")].astype(jnp.float32)
+    total = (keep_ref[...] + got).astype(jnp.bfloat16)
     for x in range(4):
         out_ref[x] = total
 

time: 73.7 us -> 73.5 us (level)
  no operation moved by 1% of the time
where the time goes in v10:
time: 73.5 us; the launch traced here: 72.7 us
  blocking collectives  67.4 us (92%)
  Pallas kernels  5.28 us (7%)
    all_to_all x1, blocking collectives, local(): lax.all_to_all(pieces.reshape(NSRC, UNIT // 2, 2, LANES), MAIN, split_axi...  49.2 us
    all_to_all x1, blocking collectives, local(): lax.all_to_all(sums.reshape(8, 2 * SITE_ROWS, LANES), FIT, split_axis=0,...  12 us
    all_gather x1, blocking collectives, local(): both = lax.all_gather(send, 'c', axis=0)  6.16 us
    pallas_call x1, Pallas kernels, make_pieces(): pl.pallas_call(piece_kernel, in_specs=[pl.BlockSpec(memory_space=pltpu.HB...  2.46 us
    pallas_call x1, Pallas kernels, make_sums(): pl.pallas_call(sum_kernel, in_specs=[pl.BlockSpec(memory_space=pltpu.VMEM...  1.74 us

profile of v10, /device:TPU:1, one launch (start us, length us, event | category | flops | bytes accessed | tf_op | source)
XLA Modules:
  0.0 72.7 jit_solution(8934273467125613177)
XLA Ops:
  0.0 2.5 %pieces.1 = bf16[5248,128]{1,0:T(8,128)(2,1)S(1)} custom-call(s32[1,5]{1,0:T(1,128)} %mu_hbm.1, s32[1,5]{1,0:T(1,128)} %bitcast.14, s32[1,5]{1,0:T(1,128)} %pos_hbm.1, bf16[5,64,4096]{2,1,0:T(8,128)(2,1)} %slab_hbm.1, bf16[32,3072]{1,0:T(8,128)(2,1)} %bitcast.13), custom_call_target="tpu_custom_call" | custom-call | flops 83886080 | bytes 4194304 | tf_op jit(solution)/shard_map/pieces/pallas_call | solution.py:84
  2.5 49.2 %all_to_all.10 = bf16[64,41,2,128]{3,2,1,0:T(2,128)(2,1)S(1)} all-to-all(bf16[64,41,2,128]{3,2,1,0:T(2,128)(2,1)S(1)} %bitcast.8), channel_id=1, replica_groups=mesh['z'=8,'yh'=4,'yl'=2,'c'=2,'x'=4] {'yl','z','yh'}, dimensions={0} | all-to-all | bytes 2686976 | tf_op jit(solution)/shard_map/all_to_all | solution.py:247
  51.7 0.0 copy-start
  51.7 1.7 %sums.1 = (f32[2,2,96,128]{3,2,1,0:T(8,128)S(1)}, bf16[2,2,96,128]{3,2,1,0:T(8,128)(2,1)S(1)}) custom-call(bf16[5248,128]{1,0:T(8,128)(2,1)S(1)} %bitcast.9), custom_call_target="tpu_custom_call" | custom-call | flops 655360 | bytes 2097152 | tf_op jit(solution)/shard_map/sums/pallas_call | solution.py:166
  53.4 6.2 %all-gather = bf16[4,2,96,128]{3,2,1,0:T(8,128)(2,1)S(1)} all-gather(bf16[2,2,96,128]{3,2,1,0:T(8,128)(2,1)S(1)} %get-tuple-element.8), channel_id=2, replica_groups=mesh['z'=8,'yh'=4,'yl'=2,'c'=2,'x'=4] {'c'}, dimensions={0}, use_global_device_ids=true | all-gather | bytes 294912 | tf_op jit(solution)/shard_map/all_gather | solution.py:251
  59.6 12.0 %all_to_all.11 = bf16[8,192,128]{2,1,0:T(8,128)(2,1)S(1)} all-to-all(bf16[8,192,128]{2,1,0:T(8,128)(2,1)S(1)} %bitcast.10), channel_id=1, replica_groups=mesh['z'=8,'yh'=4,'yl'=2,'c'=2,'x'=4] {'x','yl'}, dimensions={0} | all-to-all | bytes 786432 | tf_op jit(solution)/shard_map/all_to_all | solution.py:253
  71.7 0.0 copy-done
  71.7 1.1 %fit.1 = bf16[12,4096]{1,0:T(8,128)(2,1)} custom-call(bf16[4,4,96,128]{3,2,1,0:T(8,128)(2,1)S(1)} %bitcast.11, bf16[48,64,256]{2,1,0:T(8,128)(2,1)S(1)} %copy-done), custom_call_target="tpu_custom_call" | custom-call | tf_op jit(solution)/shard_map/fit/pallas_call | solution.py:234
  (1 shorter events, 0.0 us)
Async XLA Ops:
  51.7 20.0 %copy-start = (bf16[48,64,256]{2,1,0:T(8,128)(2,1)S(1)}, bf16[48,64,256]{2,1,0:T(8,128)(2,1)}, u32[]{:S(2)}) copy-start(bf16[48,64,256]{2,1,0:T(8,128)(2,1)} %weight_ref.1) | copy-start | bytes 4718596
